TPU v7x, 256 devices: a whole 4x4x8 slice. The times are simulated.
256 devices in a mesh: clus: 32 (over x, y, core), rhs: 8 (over z).
Axes of the slice: x: 4, y: 4, z: 8, core: 2. Of those that a mesh axis runs over, the one named last changes fastest.
Arguments:
- leaf_skel: bfloat16 [2048, 256, 64], P('clus', 'rhs'), may hold values from -6 to 6
- transfer: bfloat16 [3968, 64, 64], P('clus'), may hold values from -0.5 to 0.5
- tiles: bfloat16 [4032, 8, 64, 64], P('clus'), may hold values from -0.25 to 0.25
- cols: int32 [4032, 8], P('clus'), may hold values from -1 to 4031, as said below
Outputs:
- leaf_local: float32 [2048, 256, 64], P('clus', 'rhs')
Inputs may be any that keep to these rules, and one draw needn't show every extreme that they name: `cols`: every entry is -1 or the index of a node of the same level as its row node whose owning index along clus, the index // 126, differs from the row node's by at most 3.
All inputs are finite; a program needn't handle non-finite values.
Results may differ from a plain program's by a relative error of at most 0.0052.
Values may be sent and summed in bfloat16 or wider, within the bound.
No kernel may reach another device: no remote copies, remote signals or barrier semaphores. Data moves between devices by JAX's collectives and lax.ppermute only.
A program may use at most 128 MiB of HBM per device.

v0:
```python
import jax
import jax.numpy as jnp
from jax import lax
from jax.sharding import PartitionSpec as P

LEV = 6
REACH = 3


def passed_along(block, axis, distance):
    devices = range(lax.axis_size(axis))
    route = [(i - distance, i) for i in devices if i - distance in devices]
    return lax.ppermute(block, axis, route)


def shards(leaf_skel, transfer, tiles, cols):
    leaf_count, rhs_count, rank_width = leaf_skel.shape
    node_count = tiles.shape[0]
    top_count = leaf_count // 2 ** (LEV - 1)
    own_index = lax.axis_index("clus")
    highest = lax.Precision.HIGHEST

    def fetch(skeleton):
        pieces = []
        for offset in range(-REACH, REACH + 1):
            if offset == 0:
                pieces.append(skeleton)
            else:
                pieces.append(passed_along(skeleton, "clus", -offset))
        return (jnp.concatenate(pieces, axis=0), own_index - REACH)

    skeletons = [None] * LEV
    skeletons[LEV - 1] = leaf_skel
    views = []
    leaf_offset = top_count * (2 ** (LEV - 1) - 1)
    flat_rows, base_index = fetch(leaf_skel)
    views.append((leaf_offset, leaf_count, flat_rows, base_index, leaf_count, leaf_offset))
    for level_id in range(LEV - 2, -1, -1):
        cluster_count = top_count * 2**level_id
        first_row = top_count * (2 ** (level_id + 1) - 1) - top_count
        children = skeletons[level_id + 1].reshape(cluster_count, 2, rhs_count, rank_width)
        coeffs = transfer[first_row : first_row + 2 * cluster_count].reshape(
            cluster_count, 2, rank_width, rank_width
        )
        parent = jnp.einsum("cjrk,cjkq->crq", children, coeffs, preferred_element_type=jnp.float32)
        skeletons[level_id] = parent.astype(jnp.bfloat16)
        level_offset = top_count * (2**level_id - 1)
        flat_rows, base_index = fetch(skeletons[level_id])
        views.append(
            (level_offset, cluster_count, flat_rows, base_index, cluster_count, level_offset)
        )
    views = views[::-1]

    def couple(view):
        first_row, row_count, flat_rows, base_index, stride, row_offset = view
        column = cols[first_row : first_row + row_count]
        tile_rows = tiles[first_row : first_row + row_count]
        live_slot = column >= 0
        safe_column = jnp.maximum(column, 0)
        owner = safe_column // node_count
        local_row = safe_column % node_count
        position = jnp.where(live_slot, (owner - base_index) * stride + local_row - row_offset, 0)
        fetched = jnp.take(flat_rows, position, axis=0)
        fetched = jnp.where(live_slot[:, :, None, None], fetched, jnp.zeros((), fetched.dtype))
        return jnp.einsum("mprk,mpkq->mrq", fetched, tile_rows, preferred_element_type=jnp.float32)

    coupled = jnp.concatenate([couple(view) for view in views], axis=0)
    local_coef = coupled[0:top_count]
    for level_id in range(1, LEV):
        cluster_count = top_count * 2**level_id
        first_row = top_count * (2**level_id - 1)
        coeffs = transfer[first_row - top_count : first_row - top_count + cluster_count]
        coeffs = coeffs.reshape(cluster_count // 2, 2, rank_width, rank_width).astype(jnp.float32)
        downward = jnp.einsum("crk,cjqk->cjrq", local_coef, coeffs, precision=highest)
        downward = downward.reshape(cluster_count, rhs_count, rank_width)
        local_coef = coupled[first_row : first_row + cluster_count] + downward
    return local_coef


def solution(mesh):
    in_specs = (
        P("clus", "rhs", None),
        P("clus", None, None),
        P("clus", None, None, None),
        P("clus", None),
    )
    out_specs = P("clus", "rhs", None)
    return jax.shard_map(shards, mesh=mesh, in_specs=in_specs, out_specs=out_specs, check_vma=False)
```

profile of v0, /device:TPU:209, one launch (start us, length us, event | category | flops | bytes accessed | tf_op | source)
XLA Modules:
  0.0 330.4 jit_solution(8442709641515591790)
XLA Ops:
  34.2 9.5 %slice.69 = bf16[4,8,64,64]{0,3,2,1:T(8,128)(2,1)} slice(bf16[126,8,64,64]{0,3,2,1:T(8,128)(2,1)} %param.6), slice={[2:6], [0:8], [0:64], [0:64]} | slice | bytes 524288 | tf_op jit(solution)/shard_map/slice | solution.py:57
  43.7 9.5 %slice.66 = bf16[8,8,64,64]{0,3,2,1:T(8,128)(2,1)} slice(bf16[126,8,64,64]{0,3,2,1:T(8,128)(2,1)} %param.6), slice={[6:14], [0:8], [0:64], [0:64]} | slice | bytes 1048576 | tf_op jit(solution)/shard_map/slice | solution.py:57
  53.2 9.6 %slice.63 = bf16[16,8,64,64]{0,3,2,1:T(8,128)(2,1)} slice(bf16[126,8,64,64]{0,3,2,1:T(8,128)(2,1)} %param.6), slice={[14:30], [0:8], [0:64], [0:64]} | slice | bytes 2097152 | tf_op jit(solution)/shard_map/slice | solution.py:57
  62.8 9.6 %slice.60 = bf16[32,8,64,64]{0,3,2,1:T(8,128)(2,1)} slice(bf16[126,8,64,64]{0,3,2,1:T(8,128)(2,1)} %param.6), slice={[30:62], [0:8], [0:64], [0:64]} | slice | bytes 4194304 | tf_op jit(solution)/shard_map/slice | solution.py:57
  72.4 9.8 %slice.57 = bf16[64,8,64,64]{0,3,2,1:T(8,128)(2,1)} slice(bf16[126,8,64,64]{0,3,2,1:T(8,128)(2,1)} %param.6), slice={[62:126], [0:8], [0:64], [0:64]} | slice | bytes 8388608 | tf_op jit(solution)/shard_map/slice | solution.py:57
  82.1 7.6 %copy.65 = bf16[2,8,64,64]{3,2,1,0:T(8,128)(2,1)S(1)} copy(bf16[2,8,64,64]{0,3,2,1:T(8,128)(2,1)} %bitcast.138) | data formatting | bytes 262144 | tf_op jit(solution)/shard_map/slice | solution.py:57
  91.0 8.6 %copy.62 = bf16[4,8,64,64]{3,2,1,0:T(8,128)(2,1)} copy(bf16[4,8,64,64]{0,3,2,1:T(8,128)(2,1)} %slice.69) | data formatting | bytes 524288 | tf_op jit(solution)/shard_map/slice | solution.py:57
  100.9 8.1 %copy.59 = bf16[8,8,64,64]{3,2,1,0:T(8,128)(2,1)} copy(bf16[8,8,64,64]{0,3,2,1:T(8,128)(2,1)} %slice.66) | data formatting | bytes 1048576 | tf_op jit(solution)/shard_map/slice | solution.py:57
  110.3 8.8 %copy.56 = bf16[16,8,64,64]{3,2,1,0:T(8,128)(2,1)} copy(bf16[16,8,64,64]{0,3,2,1:T(8,128)(2,1)} %slice.63) | data formatting | bytes 2097152 | tf_op jit(solution)/shard_map/slice | solution.py:57
  120.4 10.7 %copy.53 = bf16[32,8,64,64]{3,2,1,0:T(8,128)(2,1)} copy(bf16[32,8,64,64]{0,3,2,1:T(8,128)(2,1)} %slice.60) | data formatting | bytes 4194304 | tf_op jit(solution)/shard_map/slice | solution.py:57
  132.5 13.2 %copy.72 = bf16[64,8,64,64]{3,2,1,0:T(8,128)(2,1)} copy(bf16[64,8,64,64]{0,3,2,1:T(8,128)(2,1)} %slice.57) | data formatting | bytes 8388608
  149.9 5.8 %collective-permute-start.24 = (bf16[4,32,64]{2,1,0:T(8,128)(2,1)S(1)}, bf16[4,32,64]{2,1,0:T(8,128)(2,1)S(1)}, u32[]{:S(2)}, u32[]{:S(2)}) collective-permute-start(bf16[4,32,64]{2,1,0:T(8,128)(2,1)S(1)} %fusion.36), channel_id=1, source_target_pairs={{0,24},{8,32},{16,40},{24,48},{32,56},{40,64},{48,72},{56,80},{64,... | collective-permute-start | bytes 49160 | tf_op jit(solution)/shard_map/ppermute | solution.py:13
  155.7 3.9 %collective-permute-start.25 = (bf16[4,32,64]{2,1,0:T(8,128)(2,1)S(1)}, bf16[4,32,64]{2,1,0:T(8,128)(2,1)S(1)}, u32[]{:S(2)}, u32[]{:S(2)}) collective-permute-start(bf16[4,32,64]{2,1,0:T(8,128)(2,1)S(1)} %fusion.36), channel_id=1, source_target_pairs={{0,16},{8,24},{16,32},{24,40},{32,48},{40,56},{48,64},{56,72},{64,... | collective-permute-start | bytes 49160 | tf_op jit(solution)/shard_map/ppermute | solution.py:13
  173.3 6.6 %collective-permute-start.18 = (bf16[8,32,64]{2,1,0:T(8,128)(2,1)S(1)}, bf16[8,32,64]{2,1,0:T(8,128)(2,1)S(1)}, u32[]{:S(2)}, u32[]{:S(2)}) collective-permute-start(bf16[8,32,64]{2,1,0:T(8,128)(2,1)S(1)} %fusion.33), channel_id=1, source_target_pairs={{0,24},{8,32},{16,40},{24,48},{32,56},{40,64},{48,72},{56,80},{64,... | collective-permute-start | bytes 98312 | tf_op jit(solution)/shard_map/ppermute | solution.py:13
  179.9 3.9 %collective-permute-start.19 = (bf16[8,32,64]{2,1,0:T(8,128)(2,1)S(1)}, bf16[8,32,64]{2,1,0:T(8,128)(2,1)}, u32[]{:S(2)}, u32[]{:S(2)}) collective-permute-start(bf16[8,32,64]{2,1,0:T(8,128)(2,1)S(1)} %fusion.33), channel_id=1, source_target_pairs={{0,16},{8,24},{16,32},{24,40},{32,48},{40,56},{48,64},{56,72},{64,... | collective-permute-start | bytes 98312 | tf_op jit(solution)/shard_map/ppermute | solution.py:13
  199.6 6.6 %collective-permute-start.12 = (bf16[16,32,64]{2,1,0:T(8,128)(2,1)S(1)}, bf16[16,32,64]{2,1,0:T(8,128)(2,1)}, u32[]{:S(2)}, u32[]{:S(2)}) collective-permute-start(bf16[16,32,64]{2,1,0:T(8,128)(2,1)S(1)} %fusion.30), channel_id=1, source_target_pairs={{0,24},{8,32},{16,40},{24,48},{32,56},{40,64},{48,72},{56,80},{64,... | collective-permute-start | bytes 196616 | tf_op jit(solution)/shard_map/ppermute | solution.py:13
  207.1 3.9 %collective-permute-start.13 = (bf16[16,32,64]{2,1,0:T(8,128)(2,1)S(1)}, bf16[16,32,64]{2,1,0:T(8,128)(2,1)}, u32[]{:S(2)}, u32[]{:S(2)}) collective-permute-start(bf16[16,32,64]{2,1,0:T(8,128)(2,1)S(1)} %fusion.30), channel_id=1, source_target_pairs={{0,16},{8,24},{16,32},{24,40},{32,48},{40,56},{48,64},{56,72},{64,... | collective-permute-start | bytes 196616 | tf_op jit(solution)/shard_map/ppermute | solution.py:13
  227.9 6.6 %collective-permute-start.6 = (bf16[32,32,64]{2,1,0:T(8,128)(2,1)S(1)}, bf16[32,32,64]{2,1,0:T(8,128)(2,1)S(1)}, u32[]{:S(2)}, u32[]{:S(2)}) collective-permute-start(bf16[32,32,64]{2,1,0:T(8,128)(2,1)S(1)} %fusion.27), channel_id=1, source_target_pairs={{0,24},{8,32},{16,40},{24,48},{32,56},{40,64},{48,72},{56,80},{64,... | collective-permute-start | bytes 393224 | tf_op jit(solution)/shard_map/ppermute | solution.py:13
  236.1 3.9 %collective-permute-start.7 = (bf16[32,32,64]{2,1,0:T(8,128)(2,1)S(1)}, bf16[32,32,64]{2,1,0:T(8,128)(2,1)}, u32[]{:S(2)}, u32[]{:S(2)}) collective-permute-start(bf16[32,32,64]{2,1,0:T(8,128)(2,1)S(1)} %fusion.27), channel_id=1, source_target_pairs={{0,16},{8,24},{16,32},{24,40},{32,48},{40,56},{48,64},{56,72},{64,... | collective-permute-start | bytes 393224 | tf_op jit(solution)/shard_map/ppermute | solution.py:13
  262.4 6.6 %collective-permute-start = (bf16[64,32,64]{2,1,0:T(8,128)(2,1)S(1)}, bf16[64,32,64]{2,1,0:T(8,128)(2,1)}, u32[]{:S(2)}, u32[]{:S(2)}) collective-permute-start(bf16[64,32,64]{2,1,0:T(8,128)(2,1)S(1)} %copy-done.1), channel_id=1, source_target_pairs={{0,24},{8,32},{16,40},{24,48},{32,56},{40,64},{48,72},{56,80},{64,... | collective-permute-start | bytes 786440 | tf_op jit(solution)/shard_map/ppermute | solution.py:13
  270.7 3.9 %collective-permute-start.1 = (bf16[64,32,64]{2,1,0:T(8,128)(2,1)S(1)}, bf16[64,32,64]{2,1,0:T(8,128)(2,1)}, u32[]{:S(2)}, u32[]{:S(2)}) collective-permute-start(bf16[64,32,64]{2,1,0:T(8,128)(2,1)S(1)} %copy-done.1), channel_id=1, source_target_pairs={{0,16},{8,24},{16,32},{24,40},{32,48},{40,56},{48,64},{56,72},{64,... | collective-permute-start | bytes 786440 | tf_op jit(solution)/shard_map/ppermute | solution.py:13
  310.1 7.4 %collective-permute-done.5 = bf16[64,32,64]{2,1,0:T(8,128)(2,1)S(1)} collective-permute-done((bf16[64,32,64]{2,1,0:T(8,128)(2,1)S(1)}, bf16[64,32,64]{2,1,0:T(8,128)(2,1)S(1)}, u32[]{:S(2)}, u32[]{:S(2)}) %collective-permute-start.5) | collective-permute-done | bytes 262176 | tf_op jit(solution)/shard_map/ppermute | solution.py:13
  318.4 5.3 %gather_fusion = bf16[512,32,64]{2,1,0:T(8,128)(2,1)} fusion(bf16[448,32,64]{2,1,0:T(8,128)(2,1)} %constant_dynamic-update-slice_fusion, s32[1024]{0:T(1024)S(1)} %pad_clamp_fusion.5), kind=kCustom, calls=%fused_computation | custom fusion | bytes 4196352 | tf_op jit(solution)/shard_map/jit(_take)/gather | solution.py:63
  323.7 6.6 %fusion.15 = f32[64,32,64]{2,1,0:T(8,128)} fusion(f32[64,32,64]{2,1,0:T(8,128)S(1)} %bitcast.153, bf16[64,8,64,64]{3,2,1,0:T(8,128)(2,1)} %copy.72, bf16[64,8,32,64]{3,2,1,0:T(8,128)(2,1)} %bitcast.144, pred[64,8]{1,0:T(8,128)(4,1)S(1)} %copy-done.5, pred[64,8]{1,0:T(8,128)(4,1)S(1)} %copy-done.6), kind=kOutput, calls=%fused_computation.19 | convolution fusion | flops 136445952 | bytes 7341056 | tf_op jit(solution)/shard_map/mprk,mpkq->mrq/dot_general | solution.py:65
  (190 shorter events, 153.9 us)
Async XLA Ops:
  17.7 129.4 %collective-permute-start.30 = (bf16[2,32,64]{2,1,0:T(8,128)(2,1)S(1)}, bf16[2,32,64]{2,1,0:T(8,128)(2,1)S(1)}, u32[]{:S(2)}, u32[]{:S(2)}) collective-permute-start(bf16[2,32,64]{2,1,0:T(8,128)(2,1)S(1)} %fusion.37), channel_id=1, source_target_pairs={{0,24},{8,32},{16,40},{24,48},{32,56},{40,64},{48,72},{56,80},{64,... | collective-permute-start | bytes 24584 | tf_op jit(solution)/shard_map/ppermute | solution.py:13
  21.1 128.7 %collective-permute-start.31 = (bf16[2,32,64]{2,1,0:T(8,128)(2,1)S(1)}, bf16[2,32,64]{2,1,0:T(8,128)(2,1)S(1)}, u32[]{:S(2)}, u32[]{:S(2)}) collective-permute-start(bf16[2,32,64]{2,1,0:T(8,128)(2,1)S(1)} %fusion.37), channel_id=1, source_target_pairs={{0,16},{8,24},{16,32},{24,40},{32,48},{40,56},{48,64},{56,72},{64,... | collective-permute-start | bytes 24584 | tf_op jit(solution)/shard_map/ppermute | solution.py:13
  25.0 130.7 %collective-permute-start.32 = (bf16[2,32,64]{2,1,0:T(8,128)(2,1)S(1)}, bf16[2,32,64]{2,1,0:T(8,128)(2,1)}, u32[]{:S(2)}, u32[]{:S(2)}) collective-permute-start(bf16[2,32,64]{2,1,0:T(8,128)(2,1)S(1)} %fusion.37), channel_id=1, source_target_pairs={{0,8},{8,16},{16,24},{24,32},{32,40},{40,48},{48,56},{56,64},{64,7... | collective-permute-start | bytes 24584 | tf_op jit(solution)/shard_map/ppermute | solution.py:13
  27.2 133.2 %collective-permute-start.33 = (bf16[2,32,64]{2,1,0:T(8,128)(2,1)S(1)}, bf16[2,32,64]{2,1,0:T(8,128)(2,1)}, u32[]{:S(2)}, u32[]{:S(2)}) collective-permute-start(bf16[2,32,64]{2,1,0:T(8,128)(2,1)S(1)} %fusion.37), channel_id=1, source_target_pairs={{8,0},{16,8},{24,16},{32,24},{40,32},{48,40},{56,48},{64,56},{72,6... | collective-permute-start | bytes 24584 | tf_op jit(solution)/shard_map/ppermute | solution.py:13
  29.3 134.6 %collective-permute-start.34 = (bf16[2,32,64]{2,1,0:T(8,128)(2,1)S(1)}, bf16[2,32,64]{2,1,0:T(8,128)(2,1)}, u32[]{:S(2)}, u32[]{:S(2)}) collective-permute-start(bf16[2,32,64]{2,1,0:T(8,128)(2,1)S(1)} %fusion.37), channel_id=1, source_target_pairs={{16,0},{24,8},{32,16},{40,24},{48,32},{56,40},{64,48},{72,56},{80,... | collective-permute-start | bytes 24584 | tf_op jit(solution)/shard_map/ppermute | solution.py:13
  173.3 22.9 %collective-permute-start.18 = (bf16[8,32,64]{2,1,0:T(8,128)(2,1)S(1)}, bf16[8,32,64]{2,1,0:T(8,128)(2,1)S(1)}, u32[]{:S(2)}, u32[]{:S(2)}) collective-permute-start(bf16[8,32,64]{2,1,0:T(8,128)(2,1)S(1)} %fusion.33), channel_id=1, source_target_pairs={{0,24},{8,32},{16,40},{24,48},{32,56},{40,64},{48,72},{56,80},{64,... | collective-permute-start | bytes 98312 | tf_op jit(solution)/shard_map/ppermute | solution.py:13
  188.2 23.6 %collective-permute-start.21 = (bf16[8,32,64]{2,1,0:T(8,128)(2,1)S(1)}, bf16[8,32,64]{2,1,0:T(8,128)(2,1)}, u32[]{:S(2)}, u32[]{:S(2)}) collective-permute-start(bf16[8,32,64]{2,1,0:T(8,128)(2,1)S(1)} %fusion.33), channel_id=1, source_target_pairs={{8,0},{16,8},{24,16},{32,24},{40,32},{48,40},{56,48},{64,56},{72,6... | collective-permute-start | bytes 98312 | tf_op jit(solution)/shard_map/ppermute | solution.py:13
  190.9 24.7 %collective-permute-start.22 = (bf16[8,32,64]{2,1,0:T(8,128)(2,1)S(1)}, bf16[8,32,64]{2,1,0:T(8,128)(2,1)}, u32[]{:S(2)}, u32[]{:S(2)}) collective-permute-start(bf16[8,32,64]{2,1,0:T(8,128)(2,1)S(1)} %fusion.33), channel_id=1, source_target_pairs={{16,0},{24,8},{32,16},{40,24},{48,32},{56,40},{64,48},{72,56},{80,... | collective-permute-start | bytes 98312 | tf_op jit(solution)/shard_map/ppermute | solution.py:13
  199.6 24.8 %collective-permute-start.12 = (bf16[16,32,64]{2,1,0:T(8,128)(2,1)S(1)}, bf16[16,32,64]{2,1,0:T(8,128)(2,1)}, u32[]{:S(2)}, u32[]{:S(2)}) collective-permute-start(bf16[16,32,64]{2,1,0:T(8,128)(2,1)S(1)} %fusion.30), channel_id=1, source_target_pairs={{0,24},{8,32},{16,40},{24,48},{32,56},{40,64},{48,72},{56,80},{64,... | collective-permute-start | bytes 196616 | tf_op jit(solution)/shard_map/ppermute | solution.py:13
  211.9 24.3 %collective-permute-start.14 = (bf16[16,32,64]{2,1,0:T(8,128)(2,1)S(1)}, bf16[16,32,64]{2,1,0:T(8,128)(2,1)}, u32[]{:S(2)}, u32[]{:S(2)}) collective-permute-start(bf16[16,32,64]{2,1,0:T(8,128)(2,1)S(1)} %fusion.30), channel_id=1, source_target_pairs={{0,8},{8,16},{16,24},{24,32},{32,40},{40,48},{48,56},{56,64},{64,7... | collective-permute-start | bytes 196616 | tf_op jit(solution)/shard_map/ppermute | solution.py:13
  215.6 26.6 %collective-permute-start.15 = (bf16[16,32,64]{2,1,0:T(8,128)(2,1)S(1)}, bf16[16,32,64]{2,1,0:T(8,128)(2,1)}, u32[]{:S(2)}, u32[]{:S(2)}) collective-permute-start(bf16[16,32,64]{2,1,0:T(8,128)(2,1)S(1)} %fusion.30), channel_id=1, source_target_pairs={{8,0},{16,8},{24,16},{32,24},{40,32},{48,40},{56,48},{64,56},{72,6... | collective-permute-start | bytes 196616 | tf_op jit(solution)/shard_map/ppermute | solution.py:13
  218.4 28.2 %collective-permute-start.16 = (bf16[16,32,64]{2,1,0:T(8,128)(2,1)S(1)}, bf16[16,32,64]{2,1,0:T(8,128)(2,1)}, u32[]{:S(2)}, u32[]{:S(2)}) collective-permute-start(bf16[16,32,64]{2,1,0:T(8,128)(2,1)S(1)} %fusion.30), channel_id=1, source_target_pairs={{16,0},{24,8},{32,16},{40,24},{48,32},{56,40},{64,48},{72,56},{80,... | collective-permute-start | bytes 196616 | tf_op jit(solution)/shard_map/ppermute | solution.py:13
  224.4 25.7 %collective-permute-start.17 = (bf16[16,32,64]{2,1,0:T(8,128)(2,1)S(1)}, bf16[16,32,64]{2,1,0:T(8,128)(2,1)S(1)}, u32[]{:S(2)}, u32[]{:S(2)}) collective-permute-start(bf16[16,32,64]{2,1,0:T(8,128)(2,1)S(1)} %fusion.30), channel_id=1, source_target_pairs={{24,0},{32,8},{40,16},{48,24},{56,32},{64,40},{72,48},{80,56},{88,... | collective-permute-start | bytes 196616 | tf_op jit(solution)/shard_map/ppermute | solution.py:13
  227.9 31.8 %collective-permute-start.6 = (bf16[32,32,64]{2,1,0:T(8,128)(2,1)S(1)}, bf16[32,32,64]{2,1,0:T(8,128)(2,1)S(1)}, u32[]{:S(2)}, u32[]{:S(2)}) collective-permute-start(bf16[32,32,64]{2,1,0:T(8,128)(2,1)S(1)} %fusion.27), channel_id=1, source_target_pairs={{0,24},{8,32},{16,40},{24,48},{32,56},{40,64},{48,72},{56,80},{64,... | collective-permute-start | bytes 393224 | tf_op jit(solution)/shard_map/ppermute | solution.py:13
  236.1 26.3 %collective-permute-start.7 = (bf16[32,32,64]{2,1,0:T(8,128)(2,1)S(1)}, bf16[32,32,64]{2,1,0:T(8,128)(2,1)}, u32[]{:S(2)}, u32[]{:S(2)}) collective-permute-start(bf16[32,32,64]{2,1,0:T(8,128)(2,1)S(1)} %fusion.27), channel_id=1, source_target_pairs={{0,16},{8,24},{16,32},{24,40},{32,48},{40,56},{48,64},{56,72},{64,... | collective-permute-start | bytes 393224 | tf_op jit(solution)/shard_map/ppermute | solution.py:13
  242.2 28.5 %collective-permute-start.8 = (bf16[32,32,64]{2,1,0:T(8,128)(2,1)S(1)}, bf16[32,32,64]{2,1,0:T(8,128)(2,1)}, u32[]{:S(2)}, u32[]{:S(2)}) collective-permute-start(bf16[32,32,64]{2,1,0:T(8,128)(2,1)S(1)} %fusion.27), channel_id=1, source_target_pairs={{0,8},{8,16},{16,24},{24,32},{32,40},{40,48},{48,56},{56,64},{64,7... | collective-permute-start | bytes 393224 | tf_op jit(solution)/shard_map/ppermute | solution.py:13
  246.6 30.3 %collective-permute-start.9 = (bf16[32,32,64]{2,1,0:T(8,128)(2,1)S(1)}, bf16[32,32,64]{2,1,0:T(8,128)(2,1)}, u32[]{:S(2)}, u32[]{:S(2)}) collective-permute-start(bf16[32,32,64]{2,1,0:T(8,128)(2,1)S(1)} %fusion.27), channel_id=1, source_target_pairs={{8,0},{16,8},{24,16},{32,24},{40,32},{48,40},{56,48},{64,56},{72,6... | collective-permute-start | bytes 393224 | tf_op jit(solution)/shard_map/ppermute | solution.py:13
  250.1 31.3 %collective-permute-start.10 = (bf16[32,32,64]{2,1,0:T(8,128)(2,1)S(1)}, bf16[32,32,64]{2,1,0:T(8,128)(2,1)}, u32[]{:S(2)}, u32[]{:S(2)}) collective-permute-start(bf16[32,32,64]{2,1,0:T(8,128)(2,1)S(1)} %fusion.27), channel_id=1, source_target_pairs={{16,0},{24,8},{32,16},{40,24},{48,32},{56,40},{64,48},{72,56},{80,... | collective-permute-start | bytes 393224 | tf_op jit(solution)/shard_map/ppermute | solution.py:13
  259.7 25.3 %collective-permute-start.11 = (bf16[32,32,64]{2,1,0:T(8,128)(2,1)S(1)}, bf16[32,32,64]{2,1,0:T(8,128)(2,1)S(1)}, u32[]{:S(2)}, u32[]{:S(2)}) collective-permute-start(bf16[32,32,64]{2,1,0:T(8,128)(2,1)S(1)} %fusion.27), channel_id=1, source_target_pairs={{24,0},{32,8},{40,16},{48,24},{56,32},{64,40},{72,48},{80,56},{88,... | collective-permute-start | bytes 393224 | tf_op jit(solution)/shard_map/ppermute | solution.py:13
  262.4 35.5 %collective-permute-start = (bf16[64,32,64]{2,1,0:T(8,128)(2,1)S(1)}, bf16[64,32,64]{2,1,0:T(8,128)(2,1)}, u32[]{:S(2)}, u32[]{:S(2)}) collective-permute-start(bf16[64,32,64]{2,1,0:T(8,128)(2,1)S(1)} %copy-done.1), channel_id=1, source_target_pairs={{0,24},{8,32},{16,40},{24,48},{32,56},{40,64},{48,72},{56,80},{64,... | collective-permute-start | bytes 786440 | tf_op jit(solution)/shard_map/ppermute | solution.py:13
  270.7 31.1 %collective-permute-start.1 = (bf16[64,32,64]{2,1,0:T(8,128)(2,1)S(1)}, bf16[64,32,64]{2,1,0:T(8,128)(2,1)}, u32[]{:S(2)}, u32[]{:S(2)}) collective-permute-start(bf16[64,32,64]{2,1,0:T(8,128)(2,1)S(1)} %copy-done.1), channel_id=1, source_target_pairs={{0,16},{8,24},{16,32},{24,40},{32,48},{40,56},{48,64},{56,72},{64,... | collective-permute-start | bytes 786440 | tf_op jit(solution)/shard_map/ppermute | solution.py:13
  276.9 26.7 %collective-permute-start.2 = (bf16[64,32,64]{2,1,0:T(8,128)(2,1)S(1)}, bf16[64,32,64]{2,1,0:T(8,128)(2,1)}, u32[]{:S(2)}, u32[]{:S(2)}) collective-permute-start(bf16[64,32,64]{2,1,0:T(8,128)(2,1)S(1)} %copy-done.1), channel_id=1, source_target_pairs={{0,8},{8,16},{16,24},{24,32},{32,40},{40,48},{48,56},{56,64},{64,7... | collective-permute-start | bytes 786440 | tf_op jit(solution)/shard_map/ppermute | solution.py:13
  281.4 24.9 %collective-permute-start.3 = (bf16[64,32,64]{2,1,0:T(8,128)(2,1)S(1)}, bf16[64,32,64]{2,1,0:T(8,128)(2,1)}, u32[]{:S(2)}, u32[]{:S(2)}) collective-permute-start(bf16[64,32,64]{2,1,0:T(8,128)(2,1)S(1)} %copy-done.1), channel_id=1, source_target_pairs={{8,0},{16,8},{24,16},{32,24},{40,32},{48,40},{56,48},{64,56},{72,6... | collective-permute-start | bytes 786440 | tf_op jit(solution)/shard_map/ppermute | solution.py:13
  285.0 23.2 %collective-permute-start.4 = (bf16[64,32,64]{2,1,0:T(8,128)(2,1)S(1)}, bf16[64,32,64]{2,1,0:T(8,128)(2,1)}, u32[]{:S(2)}, u32[]{:S(2)}) collective-permute-start(bf16[64,32,64]{2,1,0:T(8,128)(2,1)S(1)} %copy-done.1), channel_id=1, source_target_pairs={{16,0},{24,8},{32,16},{40,24},{48,32},{56,40},{64,48},{72,56},{80,... | collective-permute-start | bytes 786440 | tf_op jit(solution)/shard_map/ppermute | solution.py:13
  (23 other events, 451.1 us)
where the time goes:
time: 334 us; the launch traced here: 330 us
  local copies, waits for them, and re-layouts  184 us (55%)
  starting transfers between devices  111 us (33%)
  matrix products  25.5 us (8%)
  waiting for transfers between devices  7.58 us (2%)
    ppermute x36, starting transfers between devices, passed_along(): return lax.ppermute(block, axis, route)  111 us
    slice x10, local copies, waits for them, and re-layouts, couple(): tile_rows = tiles[first_row:first_row + row_count]  91.8 us
    unnamed x59, local copies, waits for them, and re-layouts  49.5 us
    dot_general x6, matrix products, couple(): jnp.einsum('mprk,mpkq->mrq', fetched, tile_rows, preferred_element_type=j...  17.3 us
    gather x6, local copies, waits for them, and re-layouts, couple(): fetched = jnp.take(flat_rows, position, axis=0)  16 us
    slice x9, local copies, waits for them, and re-layouts, shards(): transfer[first_row - top_count:first_row - top_count + cluster_count]  15.4 us
    ppermute x36, waiting for transfers between devices, passed_along(): return lax.ppermute(block, axis, route)  7.58 us
  transfers between devices with their start and end apart: 36, of which 1 were waited for; matrix products, arithmetic and copies ran while one was open for 55% of the time, Pallas kernels for 0%

commit v1 on v0

v1 whole, which is shorter than its diff:
```python
import functools

import jax
import jax.numpy as jnp
from jax import lax
from jax.experimental import pallas as pl
from jax.experimental.pallas import tpu as pltpu
from jax.sharding import PartitionSpec as P

LEV = 6
REACH = 3
SLOTS = 8
K = 64
LANES = 128
LEAF_PAIRS = 32
UPPER_PAIRS = 31
NODES = 126
ROWS = 32
MIB = 2**20
BF16 = jnp.bfloat16
F32 = jnp.float32
WHOLE = pl.BlockSpec(memory_space=pltpu.VMEM)
IN_HBM = pl.BlockSpec(memory_space=pl.ANY)
IN_SMEM = pl.BlockSpec(memory_space=pltpu.SMEM)


def pair_offset(level):
    return 2**level - 1


def params(mib):
    return pltpu.CompilerParams(vmem_limit_bytes=mib * MIB)


def pack_kernel(leaf_ref, out_ref):
    for j in range(LEAF_PAIRS):
        out_ref[j] = jnp.concatenate([leaf_ref[2 * j], leaf_ref[2 * j + 1]], axis=1)


def pack_leaves(leaf):
    return pl.pallas_call(
        pack_kernel,
        in_specs=[WHOLE],
        out_specs=WHOLE,
        out_shape=jax.ShapeDtypeStruct((LEAF_PAIRS, ROWS, LANES), BF16),
        compiler_params=params(8),
    )(leaf)


E_STRIDE = K + 1
E_NODES = NODES - 2


def upward_kernel(coeff_ref, leaf_ref, basis_ref, skel_ref, stage):
    node = lax.broadcasted_iota(jnp.int32, (E_NODES, LANES), 0)
    lane = lax.broadcasted_iota(jnp.int32, (E_NODES, LANES), 1)
    own = ((node // 2) % 2) == (lane // K)
    for a in range(K):
        slab = coeff_ref[a].astype(F32)
        twice = jnp.concatenate([slab, slab], axis=0).T
        stage[pl.ds(a, E_NODES, stride=E_STRIDE), :] = jnp.where(own, twice, 0.0)
    for g in range(E_NODES):
        basis_ref[g // 4, (g % 4) * K : (g % 4 + 1) * K, :] = stage[pl.ds(g * E_STRIDE, K), :].astype(BF16)
    for level in range(LEV - 2, -1, -1):
        first = pair_offset(level)
        below = pair_offset(level + 1)
        for i in range(2**level):
            if level == LEV - 2:
                left, right = leaf_ref[2 * i], leaf_ref[2 * i + 1]
            else:
                left, right = skel_ref[below + 2 * i], skel_ref[below + 2 * i + 1]
            children = jnp.concatenate([left, right], axis=1)
            parent = jnp.dot(children, basis_ref[first + i], preferred_element_type=F32)
            skel_ref[first + i] = parent.astype(BF16)


def upward(coeffs, leaf_pairs):
    return pl.pallas_call(
        upward_kernel,
        in_specs=[WHOLE, WHOLE],
        out_specs=(WHOLE, WHOLE),
        out_shape=(
            pltpu.VMEM((UPPER_PAIRS, 4 * K, LANES), BF16),
            jax.ShapeDtypeStruct((UPPER_PAIRS, ROWS, LANES), BF16),
        ),
        scratch_shapes=[pltpu.VMEM((E_NODES * E_STRIDE + 8, LANES), F32)],
        compiler_params=params(14),
    )(coeffs, leaf_pairs)


DEPTH = 16
CHUNKS = 4 * K // DEPTH
STRIDE = DEPTH + 1


def weights_kernel(tiles_ref, out_ref, held, stage, sem):
    per_slot = K // DEPTH

    def copy(i):
        slot, part = i // per_slot, pl.ds(i % per_slot * DEPTH, DEPTH)
        return pltpu.make_async_copy(tiles_ref.at[:, slot, part], held.at[:, slot, part], sem.at[i])

    for i in range(CHUNKS):
        copy(i).start()

    def step(i, carry):
        copy(i).wait()
        slot, base = i // per_slot, i % per_slot * DEPTH
        for k in range(DEPTH):
            slab = held[:, slot, base + k].reshape(LANES, NODES).astype(F32)
            stage[pl.ds(k, NODES, stride=STRIDE), :] = slab.T
        rows = pl.ds(pl.multiple_of(i * DEPTH, DEPTH), DEPTH)
        for g in range(NODES):
            out_ref[g, rows, :] = stage[pl.ds(g * STRIDE, DEPTH), :].astype(BF16)
        return carry

    lax.fori_loop(0, CHUNKS, step, 0)


def coupling_weights(tiles):
    slabs = jnp.transpose(tiles, (1, 2, 3, 0)).reshape(2, SLOTS // 2, K, K, NODES)
    return pl.pallas_call(
        weights_kernel,
        in_specs=[IN_HBM],
        out_specs=WHOLE,
        out_shape=pltpu.VMEM((NODES, 4 * K, LANES), BF16),
        scratch_shapes=[
            pltpu.VMEM((2, SLOTS // 2, K, K, NODES), BF16),
            pltpu.VMEM((NODES * STRIDE + 8, LANES), F32),
            pltpu.SemaphoreType.DMA((CHUNKS,)),
        ],
        compiler_params=params(22),
        cost_estimate=pl.CostEstimate(flops=0, bytes_accessed=30 * MIB, transcendentals=0),
    )(slabs)


def swap_halves(pair):
    return pltpu.roll(pair, K, 1)


def fill_table(blocks, table, pairs):
    count = 7 * pairs
    for b, block in enumerate(blocks):
        def one(i, carry):
            pair = block[i]
            table[0, b * pairs + i] = pair
            table[1, b * pairs + i] = swap_halves(pair.astype(F32)).astype(BF16)
            return carry

        lax.fori_loop(0, pairs, one, 0, unroll=4)
    for half in range(2):
        table[half, count] = jnp.zeros((ROWS, LANES), BF16)


def couple_pair(j, first_node, place_ref, table, weights_ref):
    lane = lax.broadcasted_iota(jnp.int32, (ROWS, LANES), 1)
    low = lane < K

    def fetch(slot, node):
        place = place_ref[slot, node]
        return table[place >> 12, place & 4095]

    products = []
    for side in range(2):
        node = first_node + 2 * j + side
        halves = []
        for half in range(2):
            quarter = []
            for duo in range(2):
                slot = half * 4 + duo * 2
                quarter.append(jnp.where(low, fetch(slot, node), fetch(slot + 1, node)))
            halves.append(jnp.concatenate(quarter, axis=1))
        operand = jnp.concatenate(halves, axis=0)
        products.append(jnp.dot(operand, weights_ref[node], preferred_element_type=F32))
    even, odd = products
    straight = jnp.where(low, even[:ROWS], odd[ROWS:])
    crossed = jnp.where(low, odd[:ROWS], even[ROWS:])
    return straight + swap_halves(crossed)


def upper_kernel(place_ref, *refs):
    blocks, (weights_ref, basis_ref, out_ref, table, local) = refs[:7], refs[7:]
    fill_table(blocks, table, UPPER_PAIRS)

    def one(j, carry):
        local[j] = couple_pair(j, 0, place_ref, table, weights_ref)
        return carry

    lax.fori_loop(0, UPPER_PAIRS, one, 0)
    contract = (((1,), (1,)), ((), ()))
    for level in range(LEV - 1):
        first = pair_offset(level)
        below = pair_offset(level + 1)
        for i in range(2**level):
            parent = local[first + i].astype(BF16)
            children = lax.dot_general(parent, basis_ref[first + i], contract, preferred_element_type=F32)
            for side in range(2):
                part = children[:, side * LANES : (side + 1) * LANES]
                if level == LEV - 2:
                    out_ref[2 * i + side] = part
                else:
                    local[below + 2 * i + side] += part


def upper_levels(place, blocks, weights, basis):
    return pl.pallas_call(
        upper_kernel,
        in_specs=[IN_SMEM] + [WHOLE] * 9,
        out_specs=WHOLE,
        out_shape=jax.ShapeDtypeStruct((LEAF_PAIRS, ROWS, LANES), F32),
        scratch_shapes=[
            pltpu.VMEM((2, 7 * UPPER_PAIRS + 1, ROWS, LANES), BF16),
            pltpu.VMEM((UPPER_PAIRS, ROWS, LANES), F32),
        ],
        compiler_params=params(24),
    )(place, *blocks, weights, basis)


def leaf_kernel(place_ref, *refs):
    blocks, (weights_ref, down_ref, out_ref, table) = refs[:7], refs[7:]
    fill_table(blocks, table, LEAF_PAIRS)

    def one(j, carry):
        pair = couple_pair(j, 2 * UPPER_PAIRS, place_ref, table, weights_ref) + down_ref[j]
        out_ref[2 * j] = pair[:, :K]
        out_ref[2 * j + 1] = swap_halves(pair)[:, :K]
        return carry

    lax.fori_loop(0, LEAF_PAIRS, one, 0)


def leaf_level(place, blocks, weights, down):
    return pl.pallas_call(
        leaf_kernel,
        in_specs=[IN_SMEM] + [WHOLE] * 9,
        out_specs=WHOLE,
        out_shape=jax.ShapeDtypeStruct((2 * LEAF_PAIRS, ROWS, K), F32),
        scratch_shapes=[pltpu.VMEM((2, 7 * LEAF_PAIRS + 1, ROWS, LANES), BF16)],
        compiler_params=params(24),
    )(place, *blocks, weights, down)


def places(cols, own_index):
    column = cols.T
    owner = column // NODES
    row = column - owner * NODES
    away = owner - own_index
    away = jnp.where(own_index % 2 == 0, away, -away) + REACH
    slot = lax.broadcasted_iota(jnp.int32, column.shape, 0)
    node = lax.broadcasted_iota(jnp.int32, column.shape, 1)
    is_leaf = node >= 2 * UPPER_PAIRS
    pairs = jnp.where(is_leaf, LEAF_PAIRS, UPPER_PAIRS)
    pair = jnp.where(is_leaf, row // 2 - UPPER_PAIRS, row // 2)
    swapped = (row + slot) % 2
    return jnp.where(column >= 0, away * pairs + pair + 4096 * swapped, 7 * pairs)


def shards(leaf_skel, transfer, tiles, cols):
    count = lax.axis_size("clus")
    own_index = lax.axis_index("clus")

    def moved(block, target):
        return lax.ppermute(block, "clus", [(i, target(i) % count) for i in range(count)])

    def other_core(i):
        return i ^ 1

    def outward(i):
        return i + 2 if i % 2 == 0 else i - 2

    def across(i):
        return i + 1 if i % 2 == 1 else i - 1

    place = places(cols, own_index)
    leaf = pack_leaves(leaf_skel)

    def exchange(own):
        near = moved(own, across)
        next_near = moved(own, outward)
        partner = moved(own, other_core)
        far = moved(near, outward)
        return own, near, next_near, partner, far

    def finish(own, near, next_near, partner, far):
        both = moved(jnp.concatenate([next_near, near], axis=0), other_core)
        size = own.shape[0]
        return (far, next_near, near, own, partner, both[size:], both[:size])

    leaf_parts = exchange(leaf)
    basis, upper = upward(jnp.transpose(transfer, (1, 2, 0)), leaf)
    upper_parts = exchange(upper)
    weights = coupling_weights(tiles)
    down = upper_levels(place, finish(*upper_parts), weights, basis)
    return leaf_level(place, finish(*leaf_parts), weights, down)


def solution(mesh):
    in_specs = (
        P("clus", "rhs", None),
        P("clus", None, None),
        P("clus", None, None, None),
        P("clus", None),
    )
    out_specs = P("clus", "rhs", None)
    return jax.shard_map(shards, mesh=mesh, in_specs=in_specs, out_specs=out_specs, check_vma=False)
```

time: 334 us -> 71.6 us (0.21)
  the two profiles are of different devices: /device:TPU:209 before, /device:TPU:1 now
where the time goes in v1:
time: 71.6 us; the launch traced here: 71.3 us
  Pallas kernels  38.4 us (54%)
  starting transfers between devices  20.8 us (29%)
  local copies, waits for them, and re-layouts  7.82 us (11%)
  other arithmetic  2.4 us (3%)
  waiting for transfers between devices  1.78 us (2%)
    ppermute x10, starting transfers between devices, moved(): lax.ppermute(block, 'clus', [(i, target(i) % count) for i in range(count)])  20.8 us
    pallas_call x1, Pallas kernels, leaf_level(): pl.pallas_call(leaf_kernel, in_specs=[IN_SMEM] + [WHOLE] * 9, out_specs=W...  16.2 us
    pallas_call x1, Pallas kernels, upper_levels(): pl.pallas_call(upper_kernel, in_specs=[IN_SMEM] + [WHOLE] * 9, out_specs=...  14.8 us
    unnamed x6, local copies, waits for them, and re-layouts  5.64 us
    pallas_call x1, Pallas kernels, coupling_weights(): pl.pallas_call(weights_kernel, in_specs=[IN_HBM], out_specs=WHOLE, out_sh...  5.12 us
    slice x2, local copies, waits for them, and re-layouts, finish(): return (far, next_near, near, own, partner, both[size:], both[:size])  2.19 us
    pallas_call x1, Pallas kernels, upward(): pl.pallas_call(upward_kernel, in_specs=[WHOLE, WHOLE], out_specs=(WHOLE,...  2.17 us
    ppermute x10, waiting for transfers between devices, moved(): lax.ppermute(block, 'clus', [(i, target(i) % count) for i in range(count)])  1.78 us
  transfers between devices with their start and end apart: 10, of which 1 were waited for; matrix products, arithmetic and copies ran while one was open for 6% of the time, Pallas kernels for 28%

profile of v1, /device:TPU:1, one launch (start us, length us, event | category | flops | bytes accessed | tf_op | source)
XLA Modules:
  0.0 71.3 jit_solution(4065854768924672450)
XLA Ops:
  0.0 1.0 %copy-done.2 = bf16[64,32,64]{2,1,0:T(8,128)(2,1)S(1)} copy-done((bf16[64,32,64]{2,1,0:T(8,128)(2,1)S(1)}, bf16[64,32,64]{2,1,0:T(8,128)(2,1)}, u32[]{:S(2)}) %copy-start.2) | copy-done | bytes 262168
  1.0 0.1 shard_map.46.leaf_ref.refs_3_
  1.2 0.0 copy-start.1
  1.2 1.2 %copy-done.1 = bf16[124,64,64]{0,2,1:T(8,128)(2,1)S(1)} copy-done((bf16[124,64,64]{0,2,1:T(8,128)(2,1)S(1)}, bf16[124,64,64]{0,2,1:T(8,128)(2,1)}, u32[]{:S(2)}) %copy-start.1) | copy-done | bytes 1015832
  2.4 2.2 %shard_map.48 = (bf16[31,256,128]{2,1,0:T(8,128)(2,1)S(1)}, bf16[31,32,128]{2,1,0:T(8,128)(2,1)}) custom-call(bf16[64,64,124]{2,1,0:T(8,128)(2,1)S(1)} %bitcast.33, bf16[32,32,128]{2,1,0:T(8,128)(2,1)S(1)} %shard_map.46.leaf_ref.refs_3_), custom_call_target="tpu_custom_call" | custom-call | tf_op jit(solution)/shard_map/pallas_call | solution.py:78
  4.6 2.7 %collective-permute-start.5 = (bf16[31,32,128]{2,1,0:T(8,128)(2,1)}, bf16[31,32,128]{2,1,0:T(8,128)(2,1)S(1)}, u32[]{:S(2)}, u32[]{:S(2)}) collective-permute-start(bf16[31,32,128]{2,1,0:T(8,128)(2,1)} %get-tuple-element.7.refs_3_), channel_id=1, source_target_pairs={{0,248},{8,16},{16,8},{24,32},{32,24},{40,48},{48,40},{56,64},{64,... | collective-permute-start | bytes 761864 | tf_op jit(solution)/shard_map/ppermute | solution.py:263
  7.3 5.2 %collective-permute-start.7 = (bf16[31,32,128]{2,1,0:T(8,128)(2,1)}, bf16[31,32,128]{2,1,0:T(8,128)(2,1)S(1)}, u32[]{:S(2)}, u32[]{:S(2)}) collective-permute-start(bf16[31,32,128]{2,1,0:T(8,128)(2,1)} %get-tuple-element.7.refs_3_), channel_id=1, source_target_pairs={{0,16},{8,248},{16,32},{24,8},{32,48},{40,24},{48,64},{56,40},{64,... | collective-permute-start | bytes 761864 | tf_op jit(solution)/shard_map/ppermute | solution.py:263
  12.5 2.9 %collective-permute-start.2 = (bf16[32,32,128]{2,1,0:T(8,128)(2,1)S(1)}, bf16[32,32,128]{2,1,0:T(8,128)(2,1)S(1)}, u32[]{:S(2)}, u32[]{:S(2)}) collective-permute-start(bf16[32,32,128]{2,1,0:T(8,128)(2,1)S(1)} %shard_map.46.leaf_ref.refs_3_), channel_id=1, source_target_pairs={{0,16},{8,248},{16,32},{24,8},{32,48},{40,24},{48,64},{56,40},{64,... | collective-permute-start | bytes 786440 | tf_op jit(solution)/shard_map/ppermute | solution.py:263
  15.5 1.6 %collective-permute-start.3 = (bf16[32,32,128]{2,1,0:T(8,128)(2,1)S(1)}, bf16[32,32,128]{2,1,0:T(8,128)(2,1)}, u32[]{:S(2)}, u32[]{:S(2)}) collective-permute-start(bf16[32,32,128]{2,1,0:T(8,128)(2,1)S(1)} %shard_map.46.leaf_ref.refs_3_), channel_id=1, source_target_pairs={{0,8},{8,0},{16,24},{24,16},{32,40},{40,32},{48,56},{56,48},{64,72... | collective-permute-start | bytes 786440 | tf_op jit(solution)/shard_map/ppermute | solution.py:263
  17.1 1.8 %collective-permute-done.7.refs_1_ = bf16[31,32,128]{2,1,0:T(8,128)(2,1)S(1)} collective-permute-done((bf16[31,32,128]{2,1,0:T(8,128)(2,1)}, bf16[31,32,128]{2,1,0:T(8,128)(2,1)S(1)}, u32[]{:S(2)}, u32[]{:S(2)}) %collective-permute-start.7) | collective-permute-done | bytes 253984 | tf_op jit(solution)/shard_map/ppermute | solution.py:263
  18.8 0.8 %pad_maximum_fusion.1 = bf16[62,32,128]{2,1,0:T(8,128)(2,1)} fusion(bf16[31,32,128]{2,1,0:T(8,128)(2,1)S(1)} %collective-permute-done.5.refs_2_, bf16[31,32,128]{2,1,0:T(8,128)(2,1)S(1)} %collective-permute-done.7.refs_1_), kind=kLoop, calls=%fused_computation.1 | loop fusion | flops 253952 | bytes 1015808 | tf_op jit(solution)/shard_map/concatenate | solution.py:285
  19.7 3.8 %collective-permute-start.9 = (bf16[62,32,128]{2,1,0:T(8,128)(2,1)}, bf16[62,32,128]{2,1,0:T(8,128)(2,1)}, u32[]{:S(2)}, u32[]{:S(2)}) collective-permute-start(bf16[62,32,128]{2,1,0:T(8,128)(2,1)} %pad_maximum_fusion.1), channel_id=1, source_target_pairs={{0,8},{8,0},{16,24},{24,16},{32,40},{40,32},{48,56},{56,48},{64,72... | collective-permute-start | bytes 1523720 | tf_op jit(solution)/shard_map/ppermute | solution.py:263
  23.5 0.8 %pad_maximum_fusion = bf16[64,32,128]{2,1,0:T(8,128)(2,1)} fusion(bf16[32,32,128]{2,1,0:T(8,128)(2,1)S(1)} %collective-permute-done.refs_2_, bf16[32,32,128]{2,1,0:T(8,128)(2,1)S(1)} %collective-permute-done.2.refs_1_), kind=kLoop, calls=%fused_computation | loop fusion | flops 262144 | bytes 1048576 | tf_op jit(solution)/shard_map/concatenate | solution.py:285
  24.3 2.0 %collective-permute-start.4 = (bf16[64,32,128]{2,1,0:T(8,128)(2,1)}, bf16[64,32,128]{2,1,0:T(8,128)(2,1)}, u32[]{:S(2)}, u32[]{:S(2)}) collective-permute-start(bf16[64,32,128]{2,1,0:T(8,128)(2,1)} %pad_maximum_fusion), channel_id=1, source_target_pairs={{0,8},{8,0},{16,24},{24,16},{32,40},{40,32},{48,56},{56,48},{64,72... | collective-permute-start | bytes 1572872 | tf_op jit(solution)/shard_map/ppermute | solution.py:263
  26.3 2.5 %collective-permute-start.6 = (bf16[31,32,128]{2,1,0:T(8,128)(2,1)S(1)}, bf16[31,32,128]{2,1,0:T(8,128)(2,1)S(1)}, u32[]{:S(2)}, u32[]{:S(2)}) collective-permute-start(bf16[31,32,128]{2,1,0:T(8,128)(2,1)S(1)} %collective-permute-done.5.refs_2_), channel_id=1, source_target_pairs={{0,16},{8,248},{16,32},{24,8},{32,48},{40,24},{48,64},{56,40},{64,... | collective-permute-start | bytes 761864 | tf_op jit(solution)/shard_map/ppermute | solution.py:263
  28.8 0.7 fusion.4.place_ref
  29.5 0.0 copy-start
  29.5 3.4 %copy-done = bf16[126,8,64,64]{0,3,2,1:T(8,128)(2,1)S(1)} copy-done((bf16[126,8,64,64]{0,3,2,1:T(8,128)(2,1)S(1)}, bf16[126,8,64,64]{0,3,2,1:T(8,128)(2,1)}, u32[]{:S(2)}) %copy-start) | copy-done | bytes 8257560
  32.9 5.1 %shard_map.47.refs_7_ = bf16[126,256,128]{2,1,0:T(8,128)(2,1)S(1)} custom-call(bf16[2,4,64,64,126]{4,3,2,1,0:T(8,128)(2,1)S(1)} %bitcast.32), custom_call_target="tpu_custom_call" | custom-call | bytes 31457280 | tf_op jit(solution)/shard_map/pallas_call | solution.py:122
  38.0 0.1 collective-permute-start.1
  38.1 1.1 %fusion.13 = (bf16[31,32,128]{2,1,0:T(8,128)(2,1)S(1)}, bf16[31,32,128]{2,1,0:T(8,128)(2,1)S(1)}) fusion(bf16[62,32,128]{2,1,0:T(8,128)(2,1)} %collective-permute-done.9), kind=kLoop, calls=%fused_computation.34 | loop fusion | bytes 1015808 | tf_op jit(solution)/shard_map/slice | solution.py:287
  39.2 14.8 %shard_map.49.refs_8_ = f32[32,32,128]{2,1,0:T(8,128)S(1)} custom-call(s32[8,126]{1,0:T(8,128)S(1)} %fusion.4.place_ref, bf16[31,32,128]{2,1,0:T(8,128)(2,1)S(1)} %collective-permute-done.6.refs_0_, bf16[31,32,128]{2,1,0:T(8,128)(2,1)S(1)} %collective-permute-done.7.refs_1_, bf16[31,32,128]{2,1,0:T(8,128)(2,1)S(1)} %collective-permute-done.5.refs_2_, ...), custom_call_target="tpu_custom_call" | custom-call | tf_op jit(solution)/shard_map/pallas_call | solution.py:206
  54.1 1.1 %fusion.12 = (bf16[32,32,128]{2,1,0:T(8,128)(2,1)S(1)}, bf16[32,32,128]{2,1,0:T(8,128)(2,1)S(1)}) fusion(bf16[64,32,128]{2,1,0:T(8,128)(2,1)} %collective-permute-done.4), kind=kLoop, calls=%fused_computation.33 | loop fusion | bytes 1048576 | tf_op jit(solution)/shard_map/slice | solution.py:287
  55.2 16.2 %shard_map.50 = f32[64,32,64]{2,1,0:T(8,128)} custom-call(s32[8,126]{1,0:T(8,128)S(1)} %fusion.4.place_ref, bf16[32,32,128]{2,1,0:T(8,128)(2,1)S(1)} %collective-permute-done.1.refs_0_, bf16[32,32,128]{2,1,0:T(8,128)(2,1)S(1)} %collective-permute-done.2.refs_1_, bf16[32,32,128]{2,1,0:T(8,128)(2,1)S(1)} %collective-permute-done.refs_2_, ...), custom_call_target="tpu_custom_call" | custom-call | tf_op jit(solution)/shard_map/pallas_call | solution.py:233
  (14 shorter events, 0.0 us)
Async XLA Ops:
  0.0 1.0 %copy-start.2 = (bf16[64,32,64]{2,1,0:T(8,128)(2,1)S(1)}, bf16[64,32,64]{2,1,0:T(8,128)(2,1)}, u32[]{:S(2)}) copy-start(bf16[64,32,64]{2,1,0:T(8,128)(2,1)} %leaf_ref.1) | copy-start | bytes 786436
  1.2 1.2 %copy-start.1 = (bf16[124,64,64]{0,2,1:T(8,128)(2,1)S(1)}, bf16[124,64,64]{0,2,1:T(8,128)(2,1)}, u32[]{:S(2)}) copy-start(bf16[124,64,64]{0,2,1:T(8,128)(2,1)} %param.5) | copy-start | bytes 3047428
  4.6 10.9 %collective-permute-start.5 = (bf16[31,32,128]{2,1,0:T(8,128)(2,1)}, bf16[31,32,128]{2,1,0:T(8,128)(2,1)S(1)}, u32[]{:S(2)}, u32[]{:S(2)}) collective-permute-start(bf16[31,32,128]{2,1,0:T(8,128)(2,1)} %get-tuple-element.7.refs_3_), channel_id=1, source_target_pairs={{0,248},{8,16},{16,8},{24,32},{32,24},{40,48},{48,40},{56,64},{64,... | collective-permute-start | bytes 761864 | tf_op jit(solution)/shard_map/ppermute | solution.py:263
  7.3 11.6 %collective-permute-start.7 = (bf16[31,32,128]{2,1,0:T(8,128)(2,1)}, bf16[31,32,128]{2,1,0:T(8,128)(2,1)S(1)}, u32[]{:S(2)}, u32[]{:S(2)}) collective-permute-start(bf16[31,32,128]{2,1,0:T(8,128)(2,1)} %get-tuple-element.7.refs_3_), channel_id=1, source_target_pairs={{0,16},{8,248},{16,32},{24,8},{32,48},{40,24},{48,64},{56,40},{64,... | collective-permute-start | bytes 761864 | tf_op jit(solution)/shard_map/ppermute | solution.py:263
  12.5 11.0 %collective-permute-start = (bf16[32,32,128]{2,1,0:T(8,128)(2,1)S(1)}, bf16[32,32,128]{2,1,0:T(8,128)(2,1)S(1)}, u32[]{:S(2)}, u32[]{:S(2)}) collective-permute-start(bf16[32,32,128]{2,1,0:T(8,128)(2,1)S(1)} %shard_map.46.leaf_ref.refs_3_), channel_id=1, source_target_pairs={{0,248},{8,16},{16,8},{24,32},{32,24},{40,48},{48,40},{56,64},{64,... | collective-permute-start | bytes 786440 | tf_op jit(solution)/shard_map/ppermute | solution.py:263
  12.5 11.0 %collective-permute-start.2 = (bf16[32,32,128]{2,1,0:T(8,128)(2,1)S(1)}, bf16[32,32,128]{2,1,0:T(8,128)(2,1)S(1)}, u32[]{:S(2)}, u32[]{:S(2)}) collective-permute-start(bf16[32,32,128]{2,1,0:T(8,128)(2,1)S(1)} %shard_map.46.leaf_ref.refs_3_), channel_id=1, source_target_pairs={{0,16},{8,248},{16,32},{24,8},{32,48},{40,24},{48,64},{56,40},{64,... | collective-permute-start | bytes 786440 | tf_op jit(solution)/shard_map/ppermute | solution.py:263
  15.4 23.8 %collective-permute-start.8 = (bf16[31,32,128]{2,1,0:T(8,128)(2,1)}, bf16[31,32,128]{2,1,0:T(8,128)(2,1)}, u32[]{:S(2)}, u32[]{:S(2)}) collective-permute-start(bf16[31,32,128]{2,1,0:T(8,128)(2,1)} %get-tuple-element.7.refs_3_), channel_id=1, source_target_pairs={{0,8},{8,0},{16,24},{24,16},{32,40},{40,32},{48,56},{56,48},{64,72... | collective-permute-start | bytes 761864 | tf_op jit(solution)/shard_map/ppermute | solution.py:263
  15.5 39.7 %collective-permute-start.3 = (bf16[32,32,128]{2,1,0:T(8,128)(2,1)S(1)}, bf16[32,32,128]{2,1,0:T(8,128)(2,1)}, u32[]{:S(2)}, u32[]{:S(2)}) collective-permute-start(bf16[32,32,128]{2,1,0:T(8,128)(2,1)S(1)} %shard_map.46.leaf_ref.refs_3_), channel_id=1, source_target_pairs={{0,8},{8,0},{16,24},{24,16},{32,40},{40,32},{48,56},{56,48},{64,72... | collective-permute-start | bytes 786440 | tf_op jit(solution)/shard_map/ppermute | solution.py:263
  19.7 18.3 %collective-permute-start.9 = (bf16[62,32,128]{2,1,0:T(8,128)(2,1)}, bf16[62,32,128]{2,1,0:T(8,128)(2,1)}, u32[]{:S(2)}, u32[]{:S(2)}) collective-permute-start(bf16[62,32,128]{2,1,0:T(8,128)(2,1)} %pad_maximum_fusion.1), channel_id=1, source_target_pairs={{0,8},{8,0},{16,24},{24,16},{32,40},{40,32},{48,56},{56,48},{64,72... | collective-permute-start | bytes 1523720 | tf_op jit(solution)/shard_map/ppermute | solution.py:263
  24.3 29.8 %collective-permute-start.4 = (bf16[64,32,128]{2,1,0:T(8,128)(2,1)}, bf16[64,32,128]{2,1,0:T(8,128)(2,1)}, u32[]{:S(2)}, u32[]{:S(2)}) collective-permute-start(bf16[64,32,128]{2,1,0:T(8,128)(2,1)} %pad_maximum_fusion), channel_id=1, source_target_pairs={{0,8},{8,0},{16,24},{24,16},{32,40},{40,32},{48,56},{56,48},{64,72... | collective-permute-start | bytes 1572872 | tf_op jit(solution)/shard_map/ppermute | solution.py:263
  26.3 13.0 %collective-permute-start.6 = (bf16[31,32,128]{2,1,0:T(8,128)(2,1)S(1)}, bf16[31,32,128]{2,1,0:T(8,128)(2,1)S(1)}, u32[]{:S(2)}, u32[]{:S(2)}) collective-permute-start(bf16[31,32,128]{2,1,0:T(8,128)(2,1)S(1)} %collective-permute-done.5.refs_2_), channel_id=1, source_target_pairs={{0,16},{8,248},{16,32},{24,8},{32,48},{40,24},{48,64},{56,40},{64,... | collective-permute-start | bytes 761864 | tf_op jit(solution)/shard_map/ppermute | solution.py:263
  29.5 3.4 %copy-start = (bf16[126,8,64,64]{0,3,2,1:T(8,128)(2,1)S(1)}, bf16[126,8,64,64]{0,3,2,1:T(8,128)(2,1)}, u32[]{:S(2)}) copy-start(bf16[126,8,64,64]{0,3,2,1:T(8,128)(2,1)} %param.6) | copy-start | bytes 24772612
  38.0 17.1 %collective-permute-start.1 = (bf16[32,32,128]{2,1,0:T(8,128)(2,1)S(1)}, bf16[32,32,128]{2,1,0:T(8,128)(2,1)S(1)}, u32[]{:S(2)}, u32[]{:S(2)}) collective-permute-start(bf16[32,32,128]{2,1,0:T(8,128)(2,1)S(1)} %collective-permute-done.refs_2_), channel_id=1, source_target_pairs={{0,16},{8,248},{16,32},{24,8},{32,48},{40,24},{48,64},{56,40},{64,... | collective-permute-start | bytes 786440 | tf_op jit(solution)/shard_map/ppermute | solution.py:263

commit v2 on v1

v2 whole, which is shorter than its diff:
```python
import functools

import jax
import jax.numpy as jnp
from jax import lax
from jax.experimental import pallas as pl
from jax.experimental.pallas import tpu as pltpu
from jax.sharding import PartitionSpec as P

LEV = 6
REACH = 3
SLOTS = 8
K = 64
LANES = 128
LEAF_PAIRS = 32
UPPER_PAIRS = 31
PAIRS = LEAF_PAIRS + UPPER_PAIRS
NODES = 126
ROWS = 32
MIB = 2**20
BF16 = jnp.bfloat16
F32 = jnp.float32
WHOLE = pl.BlockSpec(memory_space=pltpu.VMEM)
IN_HBM = pl.BlockSpec(memory_space=pltpu.HBM)
IN_SMEM = pl.BlockSpec(memory_space=pltpu.SMEM)


def pair_offset(level):
    return 2**level - 1


def params(mib):
    return pltpu.CompilerParams(vmem_limit_bytes=mib * MIB)


def each(count, width, body):
    def several(i, carry):
        for u in range(width):
            body(i * width + u)
        return carry

    lax.fori_loop(0, count // width, several, 0)
    for i in range(count // width * width, count):
        body(i)


def front_kernel(leaf_ref, coeff_ref, out_ref, held_ref, leaf, sems):
    first = pltpu.make_async_copy(leaf_ref, leaf, sems.at[0])
    second = pltpu.make_async_copy(coeff_ref, held_ref, sems.at[1])
    first.start()
    second.start()
    first.wait()
    for j in range(LEAF_PAIRS):
        out_ref[j] = jnp.concatenate([leaf[2 * j], leaf[2 * j + 1]], axis=1)
    second.wait()


def front(leaf, coeffs):
    return pl.pallas_call(
        front_kernel,
        in_specs=[IN_HBM, IN_HBM],
        out_specs=(WHOLE, WHOLE),
        out_shape=(pltpu.VMEM((LEAF_PAIRS, ROWS, LANES), BF16), pltpu.VMEM(coeffs.shape, BF16)),
        scratch_shapes=[pltpu.VMEM(leaf.shape, BF16), pltpu.SemaphoreType.DMA((2,))],
        compiler_params=params(60),
    )(leaf, coeffs)


E_STRIDE = K + 1
E_NODES = NODES - 2


def upward_kernel(coeff_ref, leaf_ref, basis_ref, skel_ref, stage):
    node = lax.broadcasted_iota(jnp.int32, (E_NODES, LANES), 0)
    lane = lax.broadcasted_iota(jnp.int32, (E_NODES, LANES), 1)
    own = ((node // 2) % 2) == (lane // K)
    for a in range(K):
        slab = coeff_ref[a].astype(F32)
        twice = jnp.concatenate([slab, slab], axis=0).T
        stage[pl.ds(a, E_NODES, stride=E_STRIDE), :] = jnp.where(own, twice, 0.0)
    for g in range(E_NODES):
        basis_ref[g // 4, (g % 4) * K : (g % 4 + 1) * K, :] = stage[pl.ds(g * E_STRIDE, K), :].astype(BF16)
    for level in range(LEV - 2, -1, -1):
        first = pair_offset(level)
        below = pair_offset(level + 1)
        for i in range(2**level):
            if level == LEV - 2:
                left, right = leaf_ref[2 * i], leaf_ref[2 * i + 1]
            else:
                left, right = skel_ref[below + 2 * i], skel_ref[below + 2 * i + 1]
            children = jnp.concatenate([left, right], axis=1)
            parent = jnp.dot(children, basis_ref[first + i], preferred_element_type=F32)
            skel_ref[first + i] = parent.astype(BF16)


def upward(coeffs, leaf_pairs):
    return pl.pallas_call(
        upward_kernel,
        in_specs=[WHOLE, WHOLE],
        out_specs=(WHOLE, WHOLE),
        out_shape=(
            pltpu.VMEM((UPPER_PAIRS, 4 * K, LANES), BF16),
            pltpu.VMEM((UPPER_PAIRS, ROWS, LANES), BF16),
        ),
        scratch_shapes=[pltpu.VMEM((E_NODES * E_STRIDE + 8, LANES), F32)],
        compiler_params=params(14),
    )(coeffs, leaf_pairs)


DEPTH = 16
CHUNKS = 2 * K // DEPTH
STRIDE = DEPTH + 1
DUOS = SLOTS // 4


def places(cols_ref, device_ref, place_ref):
    device = device_ref[0]
    column = cols_ref[...]
    slot = lax.broadcasted_iota(jnp.int32, column.shape, 0)
    is_leaf = lax.broadcasted_iota(jnp.int32, column.shape, 1) >= 2 * UPPER_PAIRS
    past = column - (device - REACH) * NODES
    block = jnp.zeros(column.shape, jnp.int32)
    for step in range(1, 2 * REACH + 1):
        block += jnp.where(past >= step * NODES, 1, 0)
    row = past - block * NODES
    block = jnp.where((device & 1) == 0, block, 2 * REACH - block)
    pairs = jnp.where(is_leaf, LEAF_PAIRS, UPPER_PAIRS)
    pair = (row >> 1) - jnp.where(is_leaf, UPPER_PAIRS, 0)
    swapped = (row + slot) & 1
    place_ref[...] = jnp.where(column >= 0, block * pairs + pair + 4096 * swapped, 7 * pairs)


def transpose_tiles(duo, tiles_ref, out_ref, held, stage, sem, beside):
    per_slot = K // DEPTH

    def copy(i):
        slot, part = i // per_slot, pl.ds(i % per_slot * DEPTH, DEPTH)
        return pltpu.make_async_copy(tiles_ref.at[:, 2 * duo + slot, part], held.at[:, slot, part], sem.at[i])

    for i in range(CHUNKS):
        copy(i).start()
    beside()

    def step(i, carry):
        copy(i).wait()
        slot, base = i // per_slot, i % per_slot * DEPTH
        for k in range(DEPTH):
            slab = held[:, slot, base + k].reshape(LANES, NODES).astype(F32)
            stage[pl.ds(k, NODES, stride=STRIDE), :] = slab.T
        rows = pl.ds(pl.multiple_of(i * DEPTH, DEPTH), DEPTH)
        for g in range(NODES):
            out_ref[g, rows, :] = stage[pl.ds(g * STRIDE, DEPTH), :].astype(BF16)
        return carry

    lax.fori_loop(0, CHUNKS, step, 0)


TRANSPOSE_SCRATCH = [
    pltpu.VMEM((2, 2, K, K, NODES), BF16),
    pltpu.VMEM((NODES * STRIDE + 8, LANES), F32),
    pltpu.SemaphoreType.DMA((CHUNKS,)),
]


def first_weights_kernel(tiles_ref, cols_ref, device_ref, out_ref, place_ref, held, stage, sem):
    transpose_tiles(0, tiles_ref, out_ref, held, stage, sem, lambda: places(cols_ref, device_ref, place_ref))


def first_weights(slabs, cols, device):
    return pl.pallas_call(
        first_weights_kernel,
        in_specs=[IN_HBM, WHOLE, IN_SMEM],
        out_specs=(WHOLE, WHOLE),
        out_shape=(
            pltpu.VMEM((NODES, 2 * K, LANES), BF16),
            jax.ShapeDtypeStruct((SLOTS, NODES), jnp.int32),
        ),
        scratch_shapes=TRANSPOSE_SCRATCH,
        compiler_params=params(46),
    )(slabs, cols.T, device)


def swap_halves(pair):
    return pltpu.roll(pair, K, 1)


def fill_block(table, block, number, pairs, first=0):
    for i in range(pairs):
        pair = block[first + i]
        table[0, number * pairs + i] = pair
        table[1, number * pairs + i] = swap_halves(pair)


def fill_first(own_ref, near_ref, next_ref, table_ref, sent_ref, pairs):
    for place, (number, block) in enumerate(((REACH, own_ref), (REACH - 1, near_ref), (REACH - 2, next_ref))):
        fill_block(table_ref, block, number, pairs)
        for i in range(pairs):
            sent_ref[place * pairs + i] = block[i]
    for half in range(2):
        table_ref[half, 7 * pairs] = jnp.zeros((ROWS, LANES), BF16)


def table_and_sent(pairs):
    return (
        pltpu.VMEM((2, 7 * pairs + 1, ROWS, LANES), BF16),
        pltpu.VMEM((3 * pairs, ROWS, LANES), BF16),
    )


def second_weights_kernel(tiles_ref, own_ref, near_ref, next_ref, out_ref, table_ref, sent_ref, held, stage, sem):
    def beside():
        fill_first(own_ref, near_ref, next_ref, table_ref, sent_ref, LEAF_PAIRS)

    transpose_tiles(1, tiles_ref, out_ref, held, stage, sem, beside)


def second_weights(slabs, own, near, next_near):
    return pl.pallas_call(
        second_weights_kernel,
        in_specs=[IN_HBM, WHOLE, WHOLE, WHOLE],
        out_specs=(WHOLE, WHOLE, WHOLE),
        out_shape=(pltpu.VMEM((NODES, 2 * K, LANES), BF16), *table_and_sent(LEAF_PAIRS)),
        scratch_shapes=TRANSPOSE_SCRATCH,
        compiler_params=params(38),
    )(slabs, own, near, next_near)


def upper_table_kernel(own_ref, near_ref, next_ref, table_ref, sent_ref):
    fill_first(own_ref, near_ref, next_ref, table_ref, sent_ref, UPPER_PAIRS)


def upper_table(own, near, next_near):
    return pl.pallas_call(
        upper_table_kernel,
        in_specs=[WHOLE, WHOLE, WHOLE],
        out_specs=(WHOLE, WHOLE),
        out_shape=table_and_sent(UPPER_PAIRS),
        compiler_params=params(4),
    )(own, near, next_near)


def fill_rest(table, far_ref, other_ref, pairs):
    fill_block(table, far_ref, 0, pairs)
    for step in range(REACH):
        fill_block(table, other_ref, REACH + 1 + step, pairs, step * pairs)


def couple_pair(j, first_node, place_ref, table, weights_refs):
    low = lax.broadcasted_iota(jnp.int32, (ROWS, LANES), 1) < K

    def fetch(slot, node):
        place = place_ref[slot, node]
        return table[place >> 12, place & 4095]

    products = []
    for side in range(2):
        node = first_node + 2 * j + side
        total = None
        for duo in range(DUOS):
            halves = []
            for half in range(2):
                slot = half * 4 + duo * 2
                halves.append(jnp.where(low, fetch(slot, node), fetch(slot + 1, node)))
            operand = jnp.concatenate(halves, axis=0)
            term = jnp.dot(operand, weights_refs[duo][node], preferred_element_type=F32)
            total = term if total is None else total + term
        products.append(total)
    even, odd = products
    straight = jnp.where(low, even[:ROWS], odd[ROWS:])
    crossed = jnp.where(low, odd[:ROWS], even[ROWS:])
    return straight + swap_halves(crossed)


def leaf_kernel(place_ref, far_ref, other_ref, first_ref, second_ref, given_ref, out_ref, table):
    fill_rest(table, far_ref, other_ref, LEAF_PAIRS)

    def one(j):
        out_ref[j] = couple_pair(j, 2 * UPPER_PAIRS, place_ref, table, (first_ref, second_ref))

    each(LEAF_PAIRS, 16, one)


def leaf_level(place, far, other, weights, table):
    return pl.pallas_call(
        leaf_kernel,
        in_specs=[IN_SMEM] + [WHOLE] * 5,
        out_specs=(WHOLE, WHOLE),
        out_shape=(pltpu.VMEM((LEAF_PAIRS, ROWS, LANES), F32), table_and_sent(LEAF_PAIRS)[0]),
        input_output_aliases={5: 1},
        compiler_params=params(4),
    )(place, far, other, *weights, table)[0]


def upper_kernel(place_ref, far_ref, other_ref, first_ref, second_ref, basis_ref, leaf_ref, given_ref, out_ref, table, local):
    fill_rest(table, far_ref, other_ref, UPPER_PAIRS)

    def one(j):
        local[j] = couple_pair(j, 0, place_ref, table, (first_ref, second_ref))

    each(UPPER_PAIRS, 10, one)
    contract = (((1,), (1,)), ((), ()))
    for level in range(LEV - 1):
        first = pair_offset(level)
        below = pair_offset(level + 1)
        for i in range(2**level):
            parent = local[first + i].astype(BF16)
            children = lax.dot_general(parent, basis_ref[first + i], contract, preferred_element_type=F32)
            for side in range(2):
                part = children[:, side * LANES : (side + 1) * LANES]
                if level == LEV - 2:
                    pair = part + leaf_ref[2 * i + side]
                    out_ref[4 * i + 2 * side] = pair[:, :K]
                    out_ref[4 * i + 2 * side + 1] = swap_halves(pair)[:, :K]
                else:
                    local[below + 2 * i + side] += part


def upper_levels(place, far, other, weights, basis, leaf, table):
    return pl.pallas_call(
        upper_kernel,
        in_specs=[IN_SMEM] + [WHOLE] * 7,
        out_specs=(WHOLE, WHOLE),
        out_shape=(
            jax.ShapeDtypeStruct((2 * LEAF_PAIRS, ROWS, K), F32),
            table_and_sent(UPPER_PAIRS)[0],
        ),
        input_output_aliases={7: 1},
        scratch_shapes=[pltpu.VMEM((UPPER_PAIRS, ROWS, LANES), F32)],
        compiler_params=params(6),
    )(place, far, other, *weights, basis, leaf, table)[0]


def shards(leaf_skel, transfer, tiles, cols):
    count = lax.axis_size("clus")
    own_index = lax.axis_index("clus")

    def moved(block, target):
        return lax.ppermute(block, "clus", [(i, target(i) % count) for i in range(count)])

    def other_core(i):
        return i ^ 1

    def outward(i):
        return i + 2 if i % 2 == 0 else i - 2

    def across(i):
        return i + 1 if i % 2 == 1 else i - 1

    slabs = jnp.transpose(tiles, (1, 2, 3, 0)).reshape(2, SLOTS // 2, K, K, NODES)
    leaf, coeffs = front(leaf_skel, jnp.transpose(transfer, (1, 2, 0)))
    near_leaf, next_leaf = moved(leaf, across), moved(leaf, outward)
    basis, upper = upward(coeffs, leaf)
    near_upper, next_upper = moved(upper, across), moved(upper, outward)
    slabs, upper = lax.optimization_barrier((slabs, upper))
    first, place = first_weights(slabs, cols, own_index.astype(jnp.int32).reshape(1))
    near_leaf, next_leaf, place = lax.optimization_barrier((near_leaf, next_leaf, place))
    far_leaf = moved(near_leaf, outward)
    second, leaf_table, sent_leaf = second_weights(slabs, leaf, near_leaf, next_leaf)
    other_leaf = moved(sent_leaf, other_core)
    far_upper = moved(near_upper, outward)
    table, sent_upper = upper_table(upper, near_upper, next_upper)
    other_upper = moved(sent_upper, other_core)
    weights = (first, second)
    leaf_local = leaf_level(place, far_leaf, other_leaf, weights, leaf_table)
    return upper_levels(place, far_upper, other_upper, weights, basis, leaf_local, table)


def solution(mesh):
    in_specs = (
        P("clus", "rhs", None),
        P("clus", None, None),
        P("clus", None, None, None),
        P("clus", None),
    )
    out_specs = P("clus", "rhs", None)
    return jax.shard_map(shards, mesh=mesh, in_specs=in_specs, out_specs=out_specs, check_vma=False)
```

time: 71.6 us -> 41.7 us (0.58)
  the two profiles are of different devices: /device:TPU:1 before, /device:TPU:128 now
where the time goes in v2:
time: 41.7 us; the launch traced here: 41.5 us
  Pallas kernels  20.7 us (50%)
  waiting for transfers between devices  12.2 us (29%)
  starting transfers between devices  7.87 us (19%)
  local copies, waits for them, and re-layouts  0.69 us (2%)
    ppermute x8, waiting for transfers between devices, moved(): lax.ppermute(block, 'clus', [(i, target(i) % count) for i in range(count)])  12.2 us
    ppermute x8, starting transfers between devices, moved(): lax.ppermute(block, 'clus', [(i, target(i) % count) for i in range(count)])  7.87 us
    pallas_call x1, Pallas kernels, upper_levels(): pl.pallas_call(upper_kernel, in_specs=[IN_SMEM] + [WHOLE] * 7, out_specs=...  5.07 us
    pallas_call x1, Pallas kernels, second_weights(): pl.pallas_call(second_weights_kernel, in_specs=[IN_HBM, WHOLE, WHOLE, WHO...  4.49 us
    pallas_call x1, Pallas kernels, first_weights(): pl.pallas_call(first_weights_kernel, in_specs=[IN_HBM, WHOLE, IN_SMEM], o...  3.31 us
    pallas_call x1, Pallas kernels, leaf_level(): pl.pallas_call(leaf_kernel, in_specs=[IN_SMEM] + [WHOLE] * 5, out_specs=(...  2.9 us
    pallas_call x1, Pallas kernels, upward(): pl.pallas_call(upward_kernel, in_specs=[WHOLE, WHOLE], out_specs=(WHOLE,...  2.15 us
    pallas_call x1, Pallas kernels, front(): pl.pallas_call(front_kernel, in_specs=[IN_HBM, IN_HBM], out_specs=(WHOLE,...  1.4 us
  transfers between devices with their start and end apart: 8, of which 2 were waited for; matrix products, arithmetic and copies ran while one was open for 0% of the time, Pallas kernels for 34%

profile of v2, /device:TPU:128, one launch (start us, length us, event | category | flops | bytes accessed | tf_op | source)
XLA Modules:
  0.0 41.5 jit_solution(407308139284161321)
XLA Ops:
  0.0 1.4 %shard_map.46 = (bf16[32,32,128]{2,1,0:T(8,128)(2,1)S(1)}, bf16[64,64,124]{2,1,0:T(8,128)(2,1)S(1)}) custom-call(bf16[64,32,64]{2,1,0:T(8,128)(2,1)} %leaf_ref.1, bf16[64,64,124]{2,1,0:T(8,128)(2,1)} %bitcast.9), custom_call_target="tpu_custom_call" | custom-call | tf_op jit(solution)/shard_map/pallas_call | solution.py:59
  1.4 4.7 %collective-permute-start = (bf16[32,32,128]{2,1,0:T(8,128)(2,1)S(1)}, bf16[32,32,128]{2,1,0:T(8,128)(2,1)}, u32[]{:S(2)}, u32[]{:S(2)}) collective-permute-start(bf16[32,32,128]{2,1,0:T(8,128)(2,1)S(1)} %get-tuple-element.23.leaf_ref.own_ref), channel_id=1, source_target_pairs={{0,248},{8,16},{16,8},{24,32},{32,24},{40,48},{48,40},{56,64},{64,... | collective-permute-start | bytes 786440 | tf_op jit(solution)/shard_map/ppermute | solution.py:338
  6.1 0.0 collective-permute-start.1
  6.2 2.1 %shard_map.47 = (bf16[31,256,128]{2,1,0:T(8,128)(2,1)S(1)}, bf16[31,32,128]{2,1,0:T(8,128)(2,1)}) custom-call(bf16[64,64,124]{2,1,0:T(8,128)(2,1)S(1)} %get-tuple-element.24.coeff_ref, bf16[32,32,128]{2,1,0:T(8,128)(2,1)S(1)} %get-tuple-element.23.leaf_ref.own_ref), custom_call_target="tpu_custom_call" | custom-call | tf_op jit(solution)/shard_map/pallas_call | solution.py:97
  8.3 2.0 %collective-permute-start.2 = (bf16[31,32,128]{2,1,0:T(8,128)(2,1)}, bf16[31,32,128]{2,1,0:T(8,128)(2,1)S(1)}, u32[]{:S(2)}, u32[]{:S(2)}) collective-permute-start(bf16[31,32,128]{2,1,0:T(8,128)(2,1)} %get-tuple-element.29.own_ref), channel_id=1, source_target_pairs={{0,248},{8,16},{16,8},{24,32},{32,24},{40,48},{48,40},{56,64},{64,... | collective-permute-start | bytes 761864 | tf_op jit(solution)/shard_map/ppermute | solution.py:338
  10.3 0.1 collective-permute-start.4
  10.5 0.7 %copy-done = s32[126,8]{0,1:T(8,128)S(1)} copy-done((s32[126,8]{0,1:T(8,128)S(1)}, s32[126,8]{0,1:T(8,128)}, u32[]{:S(2)}) %copy-start) | copy-done | bytes 4056
  11.2 3.3 %shard_map.48 = (bf16[126,128,128]{2,1,0:T(8,128)(2,1)S(1)}, s32[8,126]{1,0:T(8,128)S(1)}) custom-call(bf16[2,4,64,64,126]{4,3,2,1,0:T(8,128)(2,1)} %bitcast.7, s32[8,126]{1,0:T(8,128)S(1)} %bitcast.6, s32[1]{0:T(128)} %bitcast.4.device_ref), custom_call_target="tpu_custom_call" | custom-call | tf_op jit(solution)/shard_map/pallas_call | solution.py:170
  14.5 0.0 collective-permute-done.near_ref
  14.5 2.4 %collective-permute-done.1.next_ref = bf16[32,32,128]{2,1,0:T(8,128)(2,1)} collective-permute-done((bf16[32,32,128]{2,1,0:T(8,128)(2,1)S(1)}, bf16[32,32,128]{2,1,0:T(8,128)(2,1)}, u32[]{:S(2)}, u32[]{:S(2)}) %collective-permute-start.1) | collective-permute-done | bytes 262176 | tf_op jit(solution)/shard_map/ppermute | solution.py:338
  16.9 4.5 %shard_map.50 = (bf16[126,128,128]{2,1,0:T(8,128)(2,1)S(1)}, bf16[2,225,32,128]{3,2,1,0:T(8,128)(2,1)S(1)}, bf16[96,32,128]{2,1,0:T(8,128)(2,1)S(1)}) custom-call(bf16[2,4,64,64,126]{4,3,2,1,0:T(8,128)(2,1)} %bitcast.8, bf16[32,32,128]{2,1,0:T(8,128)(2,1)S(1)} %get-tuple-element.23.leaf_ref.own_ref, bf16[32,32,128]{2,1,0:T(8,128)(2,1)} %collective-permute-done.near_ref, ...), custom_call_target="tpu_custom_call" | custom-call | tf_op jit(solution)/shard_map/pallas_call | solution.py:218
  21.4 0.7 %collective-permute-start.7 = (bf16[96,32,128]{2,1,0:T(8,128)(2,1)S(1)}, bf16[96,32,128]{2,1,0:T(8,128)(2,1)S(1)}, u32[]{:S(2)}, u32[]{:S(2)}) collective-permute-start(bf16[96,32,128]{2,1,0:T(8,128)(2,1)S(1)} %get-tuple-element.36), channel_id=1, source_target_pairs={{0,8},{8,0},{16,24},{24,16},{32,40},{40,32},{48,56},{56,48},{64,72... | collective-permute-start | bytes 2359304 | tf_op jit(solution)/shard_map/ppermute | solution.py:338
  22.1 0.0 collective-permute-done.2.near_ref
  22.1 0.0 collective-permute-done.4.next_ref
  22.1 1.3 %shard_map.49 = (bf16[2,218,32,128]{3,2,1,0:T(8,128)(2,1)S(1)}, bf16[93,32,128]{2,1,0:T(8,128)(2,1)S(1)}) custom-call(bf16[31,32,128]{2,1,0:T(8,128)(2,1)} %get-tuple-element.29.own_ref, bf16[31,32,128]{2,1,0:T(8,128)(2,1)S(1)} %collective-permute-done.2.near_ref, bf16[31,32,128]{2,1,0:T(8,128)(2,1)S(1)} %collective-permute-done.4.next_ref), custom_call_target="tpu_custom_call" | custom-call | tf_op jit(solution)/shard_map/pallas_call | solution.py:233
  23.4 0.1 collective-permute-start.5
  23.6 0.1 collective-permute-start.6
  23.6 0.1 collective-permute-start.3
  23.7 9.8 %collective-permute-done.6.far_ref = bf16[32,32,128]{2,1,0:T(8,128)(2,1)S(1)} collective-permute-done((bf16[32,32,128]{2,1,0:T(8,128)(2,1)}, bf16[32,32,128]{2,1,0:T(8,128)(2,1)S(1)}, u32[]{:S(2)}, u32[]{:S(2)}) %collective-permute-start.6) | collective-permute-done | bytes 262176 | tf_op jit(solution)/shard_map/ppermute | solution.py:338
  33.5 0.0 collective-permute-done.7.other_ref
  33.5 2.9 %shard_map.51 = (f32[32,32,128]{2,1,0:T(8,128)S(1)}, bf16[2,225,32,128]{3,2,1,0:T(8,128)(2,1)S(1)}) custom-call(s32[8,126]{1,0:T(8,128)S(1)} %get-tuple-element.28.place_ref, bf16[32,32,128]{2,1,0:T(8,128)(2,1)S(1)} %collective-permute-done.6.far_ref, bf16[96,32,128]{2,1,0:T(8,128)(2,1)S(1)} %collective-permute-done.7.other_ref, ...), custom_call_target="tpu_custom_call", output_to_operand_aliasing={{1}: (5, {})} | custom-call | tf_op jit(solution)/shard_map/pallas_call | solution.py:284
  36.4 0.0 collective-permute-done.3.far_ref
  36.4 0.0 collective-permute-done.5.other_ref
  36.4 5.1 %shard_map.52 = (f32[64,32,64]{2,1,0:T(8,128)}, bf16[2,218,32,128]{3,2,1,0:T(8,128)(2,1)S(1)}) custom-call(s32[8,126]{1,0:T(8,128)S(1)} %get-tuple-element.28.place_ref, bf16[31,32,128]{2,1,0:T(8,128)(2,1)S(1)} %collective-permute-done.3.far_ref, bf16[93,32,128]{2,1,0:T(8,128)(2,1)S(1)} %collective-permute-done.5.other_ref, ...), custom_call_target="tpu_custom_call", output_to_operand_aliasing={{1}: (7, {})} | custom-call | tf_op jit(solution)/shard_map/pallas_call | solution.py:319
  (1 shorter events, 0.0 us)
Async XLA Ops:
  1.4 13.1 %collective-permute-start = (bf16[32,32,128]{2,1,0:T(8,128)(2,1)S(1)}, bf16[32,32,128]{2,1,0:T(8,128)(2,1)}, u32[]{:S(2)}, u32[]{:S(2)}) collective-permute-start(bf16[32,32,128]{2,1,0:T(8,128)(2,1)S(1)} %get-tuple-element.23.leaf_ref.own_ref), channel_id=1, source_target_pairs={{0,248},{8,16},{16,8},{24,32},{32,24},{40,48},{48,40},{56,64},{64,... | collective-permute-start | bytes 786440 | tf_op jit(solution)/shard_map/ppermute | solution.py:338
  6.1 10.8 %collective-permute-start.1 = (bf16[32,32,128]{2,1,0:T(8,128)(2,1)S(1)}, bf16[32,32,128]{2,1,0:T(8,128)(2,1)}, u32[]{:S(2)}, u32[]{:S(2)}) collective-permute-start(bf16[32,32,128]{2,1,0:T(8,128)(2,1)S(1)} %get-tuple-element.23.leaf_ref.own_ref), channel_id=1, source_target_pairs={{0,16},{8,248},{16,32},{24,8},{32,48},{40,24},{48,64},{56,40},{64,... | collective-permute-start | bytes 786440 | tf_op jit(solution)/shard_map/ppermute | solution.py:338
  8.3 13.8 %collective-permute-start.2 = (bf16[31,32,128]{2,1,0:T(8,128)(2,1)}, bf16[31,32,128]{2,1,0:T(8,128)(2,1)S(1)}, u32[]{:S(2)}, u32[]{:S(2)}) collective-permute-start(bf16[31,32,128]{2,1,0:T(8,128)(2,1)} %get-tuple-element.29.own_ref), channel_id=1, source_target_pairs={{0,248},{8,16},{16,8},{24,32},{32,24},{40,48},{48,40},{56,64},{64,... | collective-permute-start | bytes 761864 | tf_op jit(solution)/shard_map/ppermute | solution.py:338
  10.3 11.8 %collective-permute-start.4 = (bf16[31,32,128]{2,1,0:T(8,128)(2,1)}, bf16[31,32,128]{2,1,0:T(8,128)(2,1)S(1)}, u32[]{:S(2)}, u32[]{:S(2)}) collective-permute-start(bf16[31,32,128]{2,1,0:T(8,128)(2,1)} %get-tuple-element.29.own_ref), channel_id=1, source_target_pairs={{0,16},{8,248},{16,32},{24,8},{32,48},{40,24},{48,64},{56,40},{64,... | collective-permute-start | bytes 761864 | tf_op jit(solution)/shard_map/ppermute | solution.py:338
  10.5 0.7 %copy-start = (s32[126,8]{0,1:T(8,128)S(1)}, s32[126,8]{0,1:T(8,128)}, u32[]{:S(2)}) copy-start(s32[126,8]{0,1:T(8,128)} %param.7) | copy-start | bytes 12100
  21.4 12.1 %collective-permute-start.7 = (bf16[96,32,128]{2,1,0:T(8,128)(2,1)S(1)}, bf16[96,32,128]{2,1,0:T(8,128)(2,1)S(1)}, u32[]{:S(2)}, u32[]{:S(2)}) collective-permute-start(bf16[96,32,128]{2,1,0:T(8,128)(2,1)S(1)} %get-tuple-element.36), channel_id=1, source_target_pairs={{0,8},{8,0},{16,24},{24,16},{32,40},{40,32},{48,56},{56,48},{64,72... | collective-permute-start | bytes 2359304 | tf_op jit(solution)/shard_map/ppermute | solution.py:338
  23.4 13.0 %collective-permute-start.5 = (bf16[93,32,128]{2,1,0:T(8,128)(2,1)S(1)}, bf16[93,32,128]{2,1,0:T(8,128)(2,1)S(1)}, u32[]{:S(2)}, u32[]{:S(2)}) collective-permute-start(bf16[93,32,128]{2,1,0:T(8,128)(2,1)S(1)} %get-tuple-element.30), channel_id=1, source_target_pairs={{0,8},{8,0},{16,24},{24,16},{32,40},{40,32},{48,56},{56,48},{64,72... | collective-permute-start | bytes 2285576 | tf_op jit(solution)/shard_map/ppermute | solution.py:338
  23.6 10.0 %collective-permute-start.6 = (bf16[32,32,128]{2,1,0:T(8,128)(2,1)}, bf16[32,32,128]{2,1,0:T(8,128)(2,1)S(1)}, u32[]{:S(2)}, u32[]{:S(2)}) collective-permute-start(bf16[32,32,128]{2,1,0:T(8,128)(2,1)} %collective-permute-done.near_ref), channel_id=1, source_target_pairs={{0,16},{8,248},{16,32},{24,8},{32,48},{40,24},{48,64},{56,40},{64,... | collective-permute-start | bytes 786440 | tf_op jit(solution)/shard_map/ppermute | solution.py:338
  23.6 12.8 %collective-permute-start.3 = (bf16[31,32,128]{2,1,0:T(8,128)(2,1)S(1)}, bf16[31,32,128]{2,1,0:T(8,128)(2,1)S(1)}, u32[]{:S(2)}, u32[]{:S(2)}) collective-permute-start(bf16[31,32,128]{2,1,0:T(8,128)(2,1)S(1)} %collective-permute-done.2.near_ref), channel_id=1, source_target_pairs={{0,16},{8,248},{16,32},{24,8},{32,48},{40,24},{48,64},{56,40},{64,... | collective-permute-start | bytes 761864 | tf_op jit(solution)/shard_map/ppermute | solution.py:338

commit v3 on v2

--- a/solution.py
+++ b/solution.py
@@ -29,6 +29,14 @@
     return 2**level - 1
 
 
+def in_hbm(array):
+    return pltpu.with_memory_space_constraint(array, pltpu.HBM)
+
+
+def in_vmem(*arrays):
+    return tuple(pltpu.with_memory_space_constraint(array, pltpu.VMEM) for array in arrays)
+
+
 def params(mib):
     return pltpu.CompilerParams(vmem_limit_bytes=mib * MIB)
 
@@ -62,8 +70,8 @@
         out_specs=(WHOLE, WHOLE),
         out_shape=(pltpu.VMEM((LEAF_PAIRS, ROWS, LANES), BF16), pltpu.VMEM(coeffs.shape, BF16)),
         scratch_shapes=[pltpu.VMEM(leaf.shape, BF16), pltpu.SemaphoreType.DMA((2,))],
-        compiler_params=params(60),
-    )(leaf, coeffs)
+        compiler_params=params(8),
+    )(in_hbm(leaf), in_hbm(coeffs))
 
 
 E_STRIDE = K + 1
@@ -104,10 +112,10 @@
         ),
         scratch_shapes=[pltpu.VMEM((E_NODES * E_STRIDE + 8, LANES), F32)],
         compiler_params=params(14),
-    )(coeffs, leaf_pairs)
-
-
-DEPTH = 16
+    )(*in_vmem(coeffs, leaf_pairs))
+
+
+DEPTH = 32
 CHUNKS = 2 * K // DEPTH
 STRIDE = DEPTH + 1
 DUOS = SLOTS // 4
@@ -162,22 +170,25 @@
 ]
 
 
-def first_weights_kernel(tiles_ref, cols_ref, device_ref, out_ref, place_ref, held, stage, sem):
-    transpose_tiles(0, tiles_ref, out_ref, held, stage, sem, lambda: places(cols_ref, device_ref, place_ref))
+def first_weights_kernel(tiles_ref, cols_ref, device_ref, out_ref, place_ref, cols, held, stage, sem, cols_sem):
+    cols_copy = pltpu.make_async_copy(cols_ref, cols, cols_sem)
+    transpose_tiles(0, tiles_ref, out_ref, held, stage, sem, cols_copy.start)
+    cols_copy.wait()
+    places(cols, device_ref, place_ref)
 
 
 def first_weights(slabs, cols, device):
     return pl.pallas_call(
         first_weights_kernel,
-        in_specs=[IN_HBM, WHOLE, IN_SMEM],
+        in_specs=[IN_HBM, IN_HBM, IN_SMEM],
         out_specs=(WHOLE, WHOLE),
         out_shape=(
             pltpu.VMEM((NODES, 2 * K, LANES), BF16),
             jax.ShapeDtypeStruct((SLOTS, NODES), jnp.int32),
         ),
-        scratch_shapes=TRANSPOSE_SCRATCH,
-        compiler_params=params(46),
-    )(slabs, cols.T, device)
+        scratch_shapes=[pltpu.VMEM((SLOTS, NODES), jnp.int32), *TRANSPOSE_SCRATCH, pltpu.SemaphoreType.DMA],
+        compiler_params=params(12),
+    )(in_hbm(slabs), in_hbm(cols.T), device)
 
 
 def swap_halves(pair):
@@ -221,8 +232,8 @@
         out_specs=(WHOLE, WHOLE, WHOLE),
         out_shape=(pltpu.VMEM((NODES, 2 * K, LANES), BF16), *table_and_sent(LEAF_PAIRS)),
         scratch_shapes=TRANSPOSE_SCRATCH,
-        compiler_params=params(38),
-    )(slabs, own, near, next_near)
+        compiler_params=params(12),
+    )(in_hbm(slabs), *in_vmem(own, near, next_near))
 
 
 def upper_table_kernel(own_ref, near_ref, next_ref, table_ref, sent_ref):
@@ -236,7 +247,7 @@
         out_specs=(WHOLE, WHOLE),
         out_shape=table_and_sent(UPPER_PAIRS),
         compiler_params=params(4),
-    )(own, near, next_near)
+    )(*in_vmem(own, near, next_near))
 
 
 def fill_rest(table, far_ref, other_ref, pairs):
@@ -277,7 +288,7 @@
     def one(j):
         out_ref[j] = couple_pair(j, 2 * UPPER_PAIRS, place_ref, table, (first_ref, second_ref))
 
-    each(LEAF_PAIRS, 16, one)
+    each(LEAF_PAIRS, LEAF_PAIRS, one)
 
 
 def leaf_level(place, far, other, weights, table):
@@ -288,16 +299,24 @@
         out_shape=(pltpu.VMEM((LEAF_PAIRS, ROWS, LANES), F32), table_and_sent(LEAF_PAIRS)[0]),
         input_output_aliases={5: 1},
         compiler_params=params(4),
-    )(place, far, other, *weights, table)[0]
-
-
-def upper_kernel(place_ref, far_ref, other_ref, first_ref, second_ref, basis_ref, leaf_ref, given_ref, out_ref, table, local):
+    )(place, *in_vmem(far, other, *weights, table))[0]
+
+
+OUT_PARTS = 4
+OUT_STEP = LEAF_PAIRS // 2 // OUT_PARTS
+
+
+def upper_kernel(place_ref, far_ref, other_ref, first_ref, second_ref, basis_ref, leaf_ref, given_ref, out_hbm, table, local, out_ref, out_sem):
     fill_rest(table, far_ref, other_ref, UPPER_PAIRS)
 
     def one(j):
         local[j] = couple_pair(j, 0, place_ref, table, (first_ref, second_ref))
 
-    each(UPPER_PAIRS, 10, one)
+    each(UPPER_PAIRS, UPPER_PAIRS, one)
+    def put(part):
+        rows = pl.ds(part * 4 * OUT_STEP, 4 * OUT_STEP)
+        return pltpu.make_async_copy(out_ref.at[rows], out_hbm.at[rows], out_sem.at[part])
+
     contract = (((1,), (1,)), ((), ()))
     for level in range(LEV - 1):
         first = pair_offset(level)
@@ -313,21 +332,29 @@
                     out_ref[4 * i + 2 * side + 1] = swap_halves(pair)[:, :K]
                 else:
                     local[below + 2 * i + side] += part
+            if level == LEV - 2 and (i + 1) % OUT_STEP == 0:
+                put(i // OUT_STEP).start()
+    for part in range(OUT_PARTS):
+        put(part).wait()
 
 
 def upper_levels(place, far, other, weights, basis, leaf, table):
     return pl.pallas_call(
         upper_kernel,
         in_specs=[IN_SMEM] + [WHOLE] * 7,
-        out_specs=(WHOLE, WHOLE),
+        out_specs=(IN_HBM, WHOLE),
         out_shape=(
             jax.ShapeDtypeStruct((2 * LEAF_PAIRS, ROWS, K), F32),
             table_and_sent(UPPER_PAIRS)[0],
         ),
         input_output_aliases={7: 1},
-        scratch_shapes=[pltpu.VMEM((UPPER_PAIRS, ROWS, LANES), F32)],
+        scratch_shapes=[
+            pltpu.VMEM((UPPER_PAIRS, ROWS, LANES), F32),
+            pltpu.VMEM((2 * LEAF_PAIRS, ROWS, K), F32),
+            pltpu.SemaphoreType.DMA((OUT_PARTS,)),
+        ],
         compiler_params=params(6),
-    )(place, far, other, *weights, basis, leaf, table)[0]
+    )(place, *in_vmem(far, other, *weights, basis, leaf, table))[0]
 
 
 def shards(leaf_skel, transfer, tiles, cols):
@@ -351,7 +378,7 @@
     near_leaf, next_leaf = moved(leaf, across), moved(leaf, outward)
     basis, upper = upward(coeffs, leaf)
     near_upper, next_upper = moved(upper, across), moved(upper, outward)
-    slabs, upper = lax.optimization_barrier((slabs, upper))
+    cols, upper = lax.optimization_barrier((cols, upper))
     first, place = first_weights(slabs, cols, own_index.astype(jnp.int32).reshape(1))
     near_leaf, next_leaf, place = lax.optimization_barrier((near_leaf, next_leaf, place))
     far_leaf = moved(near_leaf, outward)

time: 41.7 us -> 39.6 us (0.950)
  Pallas kernels: 20.7 us -> 17.1 us
  waiting for transfers between devices: 12.2 us -> 15 us
  local copies, waits for them, and re-layouts: 0.69 us -> 0 us
  starting transfers between devices: 7.87 us -> 7.29 us
    ppermute x8, waiting for transfers between devices: 12.2 us -> 15 us  [moved(): lax.ppermute(block, 'clus', [(i, target(i) % count) for i in range(count)])]
    pallas_call x1, Pallas kernels: 4.49 us -> 3.27 us  [second_weights(): pl.pallas_call(second_weights_kernel, in_specs=[IN_HBM, WHOLE, WHOLE, WHO...]
    pallas_call x1, Pallas kernels: 5.07 us -> 4.06 us  [upper_levels(): pl.pallas_call(upper_kernel, in_specs=[IN_SMEM] + [WHOLE] * 7, out_specs=...]
    unnamed x2 -> x0, local copies, waits for them, and re-layouts: 0.69 us -> none
    pallas_call x1, Pallas kernels: 2.15 us -> 1.52 us  [upward(): pl.pallas_call(upward_kernel, in_specs=[WHOLE, WHOLE], out_specs=(WHOLE,...]
    ppermute x8, starting transfers between devices: 7.87 us -> 7.29 us  [moved(): lax.ppermute(block, 'clus', [(i, target(i) % count) for i in range(count)])]
    pallas_call x1, Pallas kernels: 2.9 us -> 2.38 us  [leaf_level(): pl.pallas_call(leaf_kernel, in_specs=[IN_SMEM] + [WHOLE] * 5, out_specs=(...]
  transfers between devices with their start and end apart: 8 -> 8, of which waited for: 2 -> 4; matrix products, arithmetic and copies ran while one was open for 0% -> 0% of each run, Pallas kernels for 34% -> 30%
where the time goes in v3:
time: 39.6 us; the launch traced here: 39.5 us
  Pallas kernels  17.1 us (43%)
  waiting for transfers between devices  15 us (38%)
  starting transfers between devices  7.29 us (18%)
    ppermute x8, waiting for transfers between devices, moved(): lax.ppermute(block, 'clus', [(i, target(i) % count) for i in range(count)])  15 us
    ppermute x8, starting transfers between devices, moved(): lax.ppermute(block, 'clus', [(i, target(i) % count) for i in range(count)])  7.29 us
    pallas_call x1, Pallas kernels, upper_levels(): pl.pallas_call(upper_kernel, in_specs=[IN_SMEM] + [WHOLE] * 7, out_specs=...  4.06 us
    pallas_call x1, Pallas kernels, second_weights(): pl.pallas_call(second_weights_kernel, in_specs=[IN_HBM, WHOLE, WHOLE, WHO...  3.27 us
    pallas_call x1, Pallas kernels, first_weights(): pl.pallas_call(first_weights_kernel, in_specs=[IN_HBM, IN_HBM, IN_SMEM],...  3.19 us
    pallas_call x1, Pallas kernels, leaf_level(): pl.pallas_call(leaf_kernel, in_specs=[IN_SMEM] + [WHOLE] * 5, out_specs=(...  2.38 us
    pallas_call x1, Pallas kernels, upward(): pl.pallas_call(upward_kernel, in_specs=[WHOLE, WHOLE], out_specs=(WHOLE,...  1.52 us
    pallas_call x1, Pallas kernels, front(): pl.pallas_call(front_kernel, in_specs=[IN_HBM, IN_HBM], out_specs=(WHOLE,...  1.4 us
  transfers between devices with their start and end apart: 8, of which 4 were waited for; matrix products, arithmetic and copies ran while one was open for 0% of the time, Pallas kernels for 30%

profile of v3, /device:TPU:128, one launch (start us, length us, event | category | flops | bytes accessed | tf_op | source)
XLA Modules:
  0.0 39.5 jit_solution(16034465169037763128)
XLA Ops:
  0.0 1.4 %shard_map.46 = (bf16[32,32,128]{2,1,0:T(8,128)(2,1)S(1)}, bf16[64,64,124]{2,1,0:T(8,128)(2,1)S(1)}) custom-call(bf16[64,32,64]{2,1,0:T(8,128)(2,1)} %leaf_ref.1, bf16[64,64,124]{2,1,0:T(8,128)(2,1)} %bitcast.8), custom_call_target="tpu_custom_call" | custom-call | tf_op jit(solution)/shard_map/pallas_call | solution.py:67
  1.4 4.7 %collective-permute-start = (bf16[32,32,128]{2,1,0:T(8,128)(2,1)S(1)}, bf16[32,32,128]{2,1,0:T(8,128)(2,1)S(1)}, u32[]{:S(2)}, u32[]{:S(2)}) collective-permute-start(bf16[32,32,128]{2,1,0:T(8,128)(2,1)S(1)} %get-tuple-element.23.leaf_ref.own_ref), channel_id=1, source_target_pairs={{0,248},{8,16},{16,8},{24,32},{32,24},{40,48},{48,40},{56,64},{64,... | collective-permute-start | bytes 786440 | tf_op jit(solution)/shard_map/ppermute | solution.py:365
  6.1 0.0 collective-permute-start.1
  6.2 1.5 %shard_map.47 = (bf16[31,256,128]{2,1,0:T(8,128)(2,1)S(1)}, bf16[31,32,128]{2,1,0:T(8,128)(2,1)S(1)}) custom-call(bf16[64,64,124]{2,1,0:T(8,128)(2,1)S(1)} %get-tuple-element.24.coeff_ref, bf16[32,32,128]{2,1,0:T(8,128)(2,1)S(1)} %get-tuple-element.23.leaf_ref.own_ref), custom_call_target="tpu_custom_call" | custom-call | tf_op jit(solution)/shard_map/pallas_call | solution.py:105
  7.7 2.0 %collective-permute-start.2 = (bf16[31,32,128]{2,1,0:T(8,128)(2,1)S(1)}, bf16[31,32,128]{2,1,0:T(8,128)(2,1)S(1)}, u32[]{:S(2)}, u32[]{:S(2)}) collective-permute-start(bf16[31,32,128]{2,1,0:T(8,128)(2,1)S(1)} %get-tuple-element.29.own_ref), channel_id=1, source_target_pairs={{0,248},{8,16},{16,8},{24,32},{32,24},{40,48},{48,40},{56,64},{64,... | collective-permute-start | bytes 761864 | tf_op jit(solution)/shard_map/ppermute | solution.py:365
  9.7 0.1 collective-permute-start.4
  9.8 3.2 %shard_map.48 = (bf16[126,128,128]{2,1,0:T(8,128)(2,1)S(1)}, s32[8,126]{1,0:T(8,128)S(1)}) custom-call(bf16[2,4,64,64,126]{4,3,2,1,0:T(8,128)(2,1)} %bitcast.6, s32[8,126]{1,0:T(8,128)} %bitcast.9, s32[1]{0:T(128)} %bitcast.4.device_ref), custom_call_target="tpu_custom_call" | custom-call | tf_op jit(solution)/shard_map/pallas_call | solution.py:181
  13.0 0.0 collective-permute-done.near_ref
  13.1 4.6 %collective-permute-done.1.next_ref = bf16[32,32,128]{2,1,0:T(8,128)(2,1)S(1)} collective-permute-done((bf16[32,32,128]{2,1,0:T(8,128)(2,1)S(1)}, bf16[32,32,128]{2,1,0:T(8,128)(2,1)S(1)}, u32[]{:S(2)}, u32[]{:S(2)}) %collective-permute-start.1) | collective-permute-done | bytes 262176 | tf_op jit(solution)/shard_map/ppermute | solution.py:365
  17.7 3.3 %shard_map.50 = (bf16[126,128,128]{2,1,0:T(8,128)(2,1)S(1)}, bf16[2,225,32,128]{3,2,1,0:T(8,128)(2,1)S(1)}, bf16[96,32,128]{2,1,0:T(8,128)(2,1)S(1)}) custom-call(bf16[2,4,64,64,126]{4,3,2,1,0:T(8,128)(2,1)} %bitcast.7, bf16[32,32,128]{2,1,0:T(8,128)(2,1)S(1)} %get-tuple-element.23.leaf_ref.own_ref, bf16[32,32,128]{2,1,0:T(8,128)(2,1)S(1)} %collective-permute-done.near_ref, ...), custom_call_target="tpu_custom_call" | custom-call | tf_op jit(solution)/shard_map/pallas_call | solution.py:229
  21.0 0.1 collective-permute-start.7
  21.1 0.0 collective-permute-done.2.near_ref
  21.1 0.3 collective-permute-done.4.next_ref
  21.4 1.3 %shard_map.49 = (bf16[2,218,32,128]{3,2,1,0:T(8,128)(2,1)S(1)}, bf16[93,32,128]{2,1,0:T(8,128)(2,1)S(1)}) custom-call(bf16[31,32,128]{2,1,0:T(8,128)(2,1)S(1)} %get-tuple-element.29.own_ref, bf16[31,32,128]{2,1,0:T(8,128)(2,1)S(1)} %collective-permute-done.2.near_ref, bf16[31,32,128]{2,1,0:T(8,128)(2,1)} %collective-permute-done.4.next_ref), custom_call_target="tpu_custom_call" | custom-call | tf_op jit(solution)/shard_map/pallas_call | solution.py:244
  22.7 0.3 collective-permute-start.5
  23.0 0.0 collective-permute-start.6
  23.0 0.0 collective-permute-start.3
  23.0 9.7 %collective-permute-done.6.far_ref = bf16[32,32,128]{2,1,0:T(8,128)(2,1)S(1)} collective-permute-done((bf16[32,32,128]{2,1,0:T(8,128)(2,1)S(1)}, bf16[32,32,128]{2,1,0:T(8,128)(2,1)S(1)}, u32[]{:S(2)}, u32[]{:S(2)}) %collective-permute-start.6) | collective-permute-done | bytes 262176 | tf_op jit(solution)/shard_map/ppermute | solution.py:365
  32.7 0.0 collective-permute-done.7.other_ref
  32.7 2.4 %shard_map.51 = (f32[32,32,128]{2,1,0:T(8,128)S(1)}, bf16[2,225,32,128]{3,2,1,0:T(8,128)(2,1)S(1)}) custom-call(s32[8,126]{1,0:T(8,128)S(1)} %get-tuple-element.28.place_ref, bf16[32,32,128]{2,1,0:T(8,128)(2,1)S(1)} %collective-permute-done.6.far_ref, bf16[96,32,128]{2,1,0:T(8,128)(2,1)S(1)} %collective-permute-done.7.other_ref, ...), custom_call_target="tpu_custom_call", output_to_operand_aliasing={{1}: (5, {})} | custom-call | tf_op jit(solution)/shard_map/pallas_call | solution.py:295
  35.1 0.3 collective-permute-done.3.far_ref
  35.4 0.0 collective-permute-done.5.other_ref
  35.4 4.1 %shard_map.52 = (f32[64,32,64]{2,1,0:T(8,128)}, bf16[2,218,32,128]{3,2,1,0:T(8,128)(2,1)S(1)}) custom-call(s32[8,126]{1,0:T(8,128)S(1)} %get-tuple-element.28.place_ref, bf16[31,32,128]{2,1,0:T(8,128)(2,1)S(1)} %collective-permute-done.3.far_ref, bf16[93,32,128]{2,1,0:T(8,128)(2,1)S(1)} %collective-permute-done.5.other_ref, ...), custom_call_target="tpu_custom_call", output_to_operand_aliasing={{1}: (7, {})} | custom-call | tf_op jit(solution)/shard_map/pallas_call | solution.py:342
Async XLA Ops:
  1.4 11.6 %collective-permute-start = (bf16[32,32,128]{2,1,0:T(8,128)(2,1)S(1)}, bf16[32,32,128]{2,1,0:T(8,128)(2,1)S(1)}, u32[]{:S(2)}, u32[]{:S(2)}) collective-permute-start(bf16[32,32,128]{2,1,0:T(8,128)(2,1)S(1)} %get-tuple-element.23.leaf_ref.own_ref), channel_id=1, source_target_pairs={{0,248},{8,16},{16,8},{24,32},{32,24},{40,48},{48,40},{56,64},{64,... | collective-permute-start | bytes 786440 | tf_op jit(solution)/shard_map/ppermute | solution.py:365
  6.1 11.5 %collective-permute-start.1 = (bf16[32,32,128]{2,1,0:T(8,128)(2,1)S(1)}, bf16[32,32,128]{2,1,0:T(8,128)(2,1)S(1)}, u32[]{:S(2)}, u32[]{:S(2)}) collective-permute-start(bf16[32,32,128]{2,1,0:T(8,128)(2,1)S(1)} %get-tuple-element.23.leaf_ref.own_ref), channel_id=1, source_target_pairs={{0,16},{8,248},{16,32},{24,8},{32,48},{40,24},{48,64},{56,40},{64,... | collective-permute-start | bytes 786440 | tf_op jit(solution)/shard_map/ppermute | solution.py:365
  7.7 13.4 %collective-permute-start.2 = (bf16[31,32,128]{2,1,0:T(8,128)(2,1)S(1)}, bf16[31,32,128]{2,1,0:T(8,128)(2,1)S(1)}, u32[]{:S(2)}, u32[]{:S(2)}) collective-permute-start(bf16[31,32,128]{2,1,0:T(8,128)(2,1)S(1)} %get-tuple-element.29.own_ref), channel_id=1, source_target_pairs={{0,248},{8,16},{16,8},{24,32},{32,24},{40,48},{48,40},{56,64},{64,... | collective-permute-start | bytes 761864 | tf_op jit(solution)/shard_map/ppermute | solution.py:365
  9.7 11.7 %collective-permute-start.4 = (bf16[31,32,128]{2,1,0:T(8,128)(2,1)S(1)}, bf16[31,32,128]{2,1,0:T(8,128)(2,1)}, u32[]{:S(2)}, u32[]{:S(2)}) collective-permute-start(bf16[31,32,128]{2,1,0:T(8,128)(2,1)S(1)} %get-tuple-element.29.own_ref), channel_id=1, source_target_pairs={{0,16},{8,248},{16,32},{24,8},{32,48},{40,24},{48,64},{56,40},{64,... | collective-permute-start | bytes 761864 | tf_op jit(solution)/shard_map/ppermute | solution.py:365
  21.0 11.7 %collective-permute-start.7 = (bf16[96,32,128]{2,1,0:T(8,128)(2,1)S(1)}, bf16[96,32,128]{2,1,0:T(8,128)(2,1)S(1)}, u32[]{:S(2)}, u32[]{:S(2)}) collective-permute-start(bf16[96,32,128]{2,1,0:T(8,128)(2,1)S(1)} %get-tuple-element.36), channel_id=1, source_target_pairs={{0,8},{8,0},{16,24},{24,16},{32,40},{40,32},{48,56},{56,48},{64,72... | collective-permute-start | bytes 2359304 | tf_op jit(solution)/shard_map/ppermute | solution.py:365
  22.7 12.7 %collective-permute-start.5 = (bf16[93,32,128]{2,1,0:T(8,128)(2,1)S(1)}, bf16[93,32,128]{2,1,0:T(8,128)(2,1)S(1)}, u32[]{:S(2)}, u32[]{:S(2)}) collective-permute-start(bf16[93,32,128]{2,1,0:T(8,128)(2,1)S(1)} %get-tuple-element.30), channel_id=1, source_target_pairs={{0,8},{8,0},{16,24},{24,16},{32,40},{40,32},{48,56},{56,48},{64,72... | collective-permute-start | bytes 2285576 | tf_op jit(solution)/shard_map/ppermute | solution.py:365
  23.0 9.7 %collective-permute-start.6 = (bf16[32,32,128]{2,1,0:T(8,128)(2,1)S(1)}, bf16[32,32,128]{2,1,0:T(8,128)(2,1)S(1)}, u32[]{:S(2)}, u32[]{:S(2)}) collective-permute-start(bf16[32,32,128]{2,1,0:T(8,128)(2,1)S(1)} %collective-permute-done.near_ref), channel_id=1, source_target_pairs={{0,16},{8,248},{16,32},{24,8},{32,48},{40,24},{48,64},{56,40},{64,... | collective-permute-start | bytes 786440 | tf_op jit(solution)/shard_map/ppermute | solution.py:365
  23.0 12.4 %collective-permute-start.3 = (bf16[31,32,128]{2,1,0:T(8,128)(2,1)S(1)}, bf16[31,32,128]{2,1,0:T(8,128)(2,1)S(1)}, u32[]{:S(2)}, u32[]{:S(2)}) collective-permute-start(bf16[31,32,128]{2,1,0:T(8,128)(2,1)S(1)} %collective-permute-done.2.near_ref), channel_id=1, source_target_pairs={{0,16},{8,248},{16,32},{24,8},{32,48},{40,24},{48,64},{56,40},{64,... | collective-permute-start | bytes 761864 | tf_op jit(solution)/shard_map/ppermute | solution.py:365

commit v4 on v3

--- a/solution.py
+++ b/solution.py
@@ -250,10 +250,21 @@
     )(*in_vmem(own, near, next_near))
 
 
-def fill_rest(table, far_ref, other_ref, pairs):
-    fill_block(table, far_ref, 0, pairs)
-    for step in range(REACH):
-        fill_block(table, other_ref, REACH + 1 + step, pairs, step * pairs)
+def rest_kernel(leaf_ref, upper_ref, given_leaf, given_upper, leaf_table, upper_table):
+    for table, other_ref, pairs in ((leaf_table, leaf_ref, LEAF_PAIRS), (upper_table, upper_ref, UPPER_PAIRS)):
+        for step in range(REACH):
+            fill_block(table, other_ref, REACH + 1 + step, pairs, step * pairs)
+
+
+def rest_of_tables(other_leaf, other_upper, leaf_table, table):
+    return pl.pallas_call(
+        rest_kernel,
+        in_specs=[WHOLE] * 4,
+        out_specs=(WHOLE, WHOLE),
+        out_shape=(table_and_sent(LEAF_PAIRS)[0], table_and_sent(UPPER_PAIRS)[0]),
+        input_output_aliases={2: 0, 3: 1},
+        compiler_params=params(2),
+    )(*in_vmem(other_leaf, other_upper, leaf_table, table))
 
 
 def couple_pair(j, first_node, place_ref, table, weights_refs):
@@ -282,8 +293,8 @@
     return straight + swap_halves(crossed)
 
 
-def leaf_kernel(place_ref, far_ref, other_ref, first_ref, second_ref, given_ref, out_ref, table):
-    fill_rest(table, far_ref, other_ref, LEAF_PAIRS)
+def leaf_kernel(place_ref, far_ref, first_ref, second_ref, given_ref, out_ref, table):
+    fill_block(table, far_ref, 0, LEAF_PAIRS)
 
     def one(j):
         out_ref[j] = couple_pair(j, 2 * UPPER_PAIRS, place_ref, table, (first_ref, second_ref))
@@ -291,23 +302,23 @@
     each(LEAF_PAIRS, LEAF_PAIRS, one)
 
 
-def leaf_level(place, far, other, weights, table):
+def leaf_level(place, far, weights, table):
     return pl.pallas_call(
         leaf_kernel,
-        in_specs=[IN_SMEM] + [WHOLE] * 5,
+        in_specs=[IN_SMEM] + [WHOLE] * 4,
         out_specs=(WHOLE, WHOLE),
         out_shape=(pltpu.VMEM((LEAF_PAIRS, ROWS, LANES), F32), table_and_sent(LEAF_PAIRS)[0]),
-        input_output_aliases={5: 1},
+        input_output_aliases={4: 1},
         compiler_params=params(4),
-    )(place, *in_vmem(far, other, *weights, table))[0]
+    )(place, *in_vmem(far, *weights, table))[0]
 
 
 OUT_PARTS = 4
 OUT_STEP = LEAF_PAIRS // 2 // OUT_PARTS
 
 
-def upper_kernel(place_ref, far_ref, other_ref, first_ref, second_ref, basis_ref, leaf_ref, given_ref, out_hbm, table, local, out_ref, out_sem):
-    fill_rest(table, far_ref, other_ref, UPPER_PAIRS)
+def upper_kernel(place_ref, far_ref, first_ref, second_ref, basis_ref, leaf_ref, given_ref, out_hbm, table, local, out_ref, out_sem):
+    fill_block(table, far_ref, 0, UPPER_PAIRS)
 
     def one(j):
         local[j] = couple_pair(j, 0, place_ref, table, (first_ref, second_ref))
@@ -338,23 +349,23 @@
         put(part).wait()
 
 
-def upper_levels(place, far, other, weights, basis, leaf, table):
+def upper_levels(place, far, weights, basis, leaf, table):
     return pl.pallas_call(
         upper_kernel,
-        in_specs=[IN_SMEM] + [WHOLE] * 7,
+        in_specs=[IN_SMEM] + [WHOLE] * 6,
         out_specs=(IN_HBM, WHOLE),
         out_shape=(
             jax.ShapeDtypeStruct((2 * LEAF_PAIRS, ROWS, K), F32),
             table_and_sent(UPPER_PAIRS)[0],
         ),
-        input_output_aliases={7: 1},
+        input_output_aliases={6: 1},
         scratch_shapes=[
             pltpu.VMEM((UPPER_PAIRS, ROWS, LANES), F32),
             pltpu.VMEM((2 * LEAF_PAIRS, ROWS, K), F32),
             pltpu.SemaphoreType.DMA((OUT_PARTS,)),
         ],
         compiler_params=params(6),
-    )(place, *in_vmem(far, other, *weights, basis, leaf, table))[0]
+    )(place, *in_vmem(far, *weights, basis, leaf, table))[0]
 
 
 def shards(leaf_skel, transfer, tiles, cols):
@@ -387,9 +398,10 @@
     far_upper = moved(near_upper, outward)
     table, sent_upper = upper_table(upper, near_upper, next_upper)
     other_upper = moved(sent_upper, other_core)
+    leaf_table, table = rest_of_tables(other_leaf, other_upper, leaf_table, table)
     weights = (first, second)
-    leaf_local = leaf_level(place, far_leaf, other_leaf, weights, leaf_table)
-    return upper_levels(place, far_upper, other_upper, weights, basis, leaf_local, table)
+    leaf_local = leaf_level(place, far_leaf, weights, leaf_table)
+    return upper_levels(place, far_upper, weights, basis, leaf_local, table)
 
 
 def solution(mesh):

time: 39.6 us -> 38.5 us (0.972)
  waiting for transfers between devices: 15 us -> 13.3 us
    ppermute x8, waiting for transfers between devices: 15 us -> 13.3 us  [moved(): lax.ppermute(block, 'clus', [(i, target(i) % count) for i in range(count)])]
    pallas_call x2 -> x3, Pallas kernels: 6.45 us -> 6.58 us  [the longest x1 3.81 us: upper_levels(): pl.pallas_call(upper_kernel, in_specs=[IN_SMEM] + [WHOLE] * 6, out_specs=...]
  transfers between devices with their start and end apart: 8 -> 8, of which waited for: 4 -> 6; matrix products, arithmetic and copies ran while one was open for 0% -> 0% of each run, Pallas kernels for 30% -> 31%
where the time goes in v4:
time: 38.5 us; the launch traced here: 38.4 us
  Pallas kernels  17.3 us (45%)
  waiting for transfers between devices  13.3 us (35%)
  starting transfers between devices  7.55 us (20%)
    ppermute x8, waiting for transfers between devices, moved(): lax.ppermute(block, 'clus', [(i, target(i) % count) for i in range(count)])  13.3 us
    ppermute x8, starting transfers between devices, moved(): lax.ppermute(block, 'clus', [(i, target(i) % count) for i in range(count)])  7.55 us
    pallas_call x1, Pallas kernels, upper_levels(): pl.pallas_call(upper_kernel, in_specs=[IN_SMEM] + [WHOLE] * 6, out_specs=...  3.81 us
    pallas_call x1, Pallas kernels, second_weights(): pl.pallas_call(second_weights_kernel, in_specs=[IN_HBM, WHOLE, WHOLE, WHO...  3.27 us
    pallas_call x1, Pallas kernels, first_weights(): pl.pallas_call(first_weights_kernel, in_specs=[IN_HBM, IN_HBM, IN_SMEM],...  3.19 us
    pallas_call x1, Pallas kernels, leaf_level(): pl.pallas_call(leaf_kernel, in_specs=[IN_SMEM] + [WHOLE] * 4, out_specs=(...  2.16 us
    pallas_call x1, Pallas kernels, upward(): pl.pallas_call(upward_kernel, in_specs=[WHOLE, WHOLE], out_specs=(WHOLE,...  1.52 us
    pallas_call x1, Pallas kernels, front(): pl.pallas_call(front_kernel, in_specs=[IN_HBM, IN_HBM], out_specs=(WHOLE,...  1.4 us
  transfers between devices with their start and end apart: 8, of which 6 were waited for; matrix products, arithmetic and copies ran while one was open for 0% of the time, Pallas kernels for 31%

profile of v4, /device:TPU:128, one launch (start us, length us, event | category | flops | bytes accessed | tf_op | source)
XLA Modules:
  0.0 38.4 jit_solution(15492157896849200239)
XLA Ops:
  0.0 1.4 %shard_map.46 = (bf16[32,32,128]{2,1,0:T(8,128)(2,1)S(1)}, bf16[64,64,124]{2,1,0:T(8,128)(2,1)S(1)}) custom-call(bf16[64,32,64]{2,1,0:T(8,128)(2,1)} %leaf_ref.1, bf16[64,64,124]{2,1,0:T(8,128)(2,1)} %bitcast.8), custom_call_target="tpu_custom_call" | custom-call | tf_op jit(solution)/shard_map/pallas_call | solution.py:67
  1.4 1.7 %collective-permute-start.1 = (bf16[32,32,128]{2,1,0:T(8,128)(2,1)S(1)}, bf16[32,32,128]{2,1,0:T(8,128)(2,1)S(1)}, u32[]{:S(2)}, u32[]{:S(2)}) collective-permute-start(bf16[32,32,128]{2,1,0:T(8,128)(2,1)S(1)} %get-tuple-element.25.leaf_ref.own_ref), channel_id=1, source_target_pairs={{0,16},{8,248},{16,32},{24,8},{32,48},{40,24},{48,64},{56,40},{64,... | collective-permute-start | bytes 786440 | tf_op jit(solution)/shard_map/ppermute | solution.py:376
  3.1 3.5 %collective-permute-start = (bf16[32,32,128]{2,1,0:T(8,128)(2,1)S(1)}, bf16[32,32,128]{2,1,0:T(8,128)(2,1)S(1)}, u32[]{:S(2)}, u32[]{:S(2)}) collective-permute-start(bf16[32,32,128]{2,1,0:T(8,128)(2,1)S(1)} %get-tuple-element.25.leaf_ref.own_ref), channel_id=1, source_target_pairs={{0,248},{8,16},{16,8},{24,32},{32,24},{40,48},{48,40},{56,64},{64,... | collective-permute-start | bytes 786440 | tf_op jit(solution)/shard_map/ppermute | solution.py:376
  6.6 1.5 %shard_map.47 = (bf16[31,256,128]{2,1,0:T(8,128)(2,1)S(1)}, bf16[31,32,128]{2,1,0:T(8,128)(2,1)S(1)}) custom-call(bf16[64,64,124]{2,1,0:T(8,128)(2,1)S(1)} %get-tuple-element.26.coeff_ref, bf16[32,32,128]{2,1,0:T(8,128)(2,1)S(1)} %get-tuple-element.25.leaf_ref.own_ref), custom_call_target="tpu_custom_call" | custom-call | tf_op jit(solution)/shard_map/pallas_call | solution.py:105
  8.1 1.3 %collective-permute-start.6 = (bf16[31,32,128]{2,1,0:T(8,128)(2,1)S(1)}, bf16[31,32,128]{2,1,0:T(8,128)(2,1)}, u32[]{:S(2)}, u32[]{:S(2)}) collective-permute-start(bf16[31,32,128]{2,1,0:T(8,128)(2,1)S(1)} %get-tuple-element.37.own_ref), channel_id=1, source_target_pairs={{0,16},{8,248},{16,32},{24,8},{32,48},{40,24},{48,64},{56,40},{64,... | collective-permute-start | bytes 761864 | tf_op jit(solution)/shard_map/ppermute | solution.py:376
  9.4 0.4 %collective-permute-start.2 = (bf16[31,32,128]{2,1,0:T(8,128)(2,1)S(1)}, bf16[31,32,128]{2,1,0:T(8,128)(2,1)S(1)}, u32[]{:S(2)}, u32[]{:S(2)}) collective-permute-start(bf16[31,32,128]{2,1,0:T(8,128)(2,1)S(1)} %get-tuple-element.37.own_ref), channel_id=1, source_target_pairs={{0,248},{8,16},{16,8},{24,32},{32,24},{40,48},{48,40},{56,64},{64,... | collective-permute-start | bytes 761864 | tf_op jit(solution)/shard_map/ppermute | solution.py:376
  9.8 3.2 %shard_map.48 = (bf16[126,128,128]{2,1,0:T(8,128)(2,1)S(1)}, s32[8,126]{1,0:T(8,128)S(1)}) custom-call(bf16[2,4,64,64,126]{4,3,2,1,0:T(8,128)(2,1)} %bitcast.6, s32[8,126]{1,0:T(8,128)} %bitcast.9, s32[1]{0:T(128)} %bitcast.4.device_ref), custom_call_target="tpu_custom_call" | custom-call | tf_op jit(solution)/shard_map/pallas_call | solution.py:181
  13.0 0.0 collective-permute-done.1.next_ref
  13.1 0.9 %collective-permute-done.near_ref = bf16[32,32,128]{2,1,0:T(8,128)(2,1)S(1)} collective-permute-done((bf16[32,32,128]{2,1,0:T(8,128)(2,1)S(1)}, bf16[32,32,128]{2,1,0:T(8,128)(2,1)S(1)}, u32[]{:S(2)}, u32[]{:S(2)}) %collective-permute-start) | collective-permute-done | bytes 262176 | tf_op jit(solution)/shard_map/ppermute | solution.py:376
  14.0 3.3 %shard_map.49 = (bf16[126,128,128]{2,1,0:T(8,128)(2,1)S(1)}, bf16[2,225,32,128]{3,2,1,0:T(8,128)(2,1)S(1)}, bf16[96,32,128]{2,1,0:T(8,128)(2,1)S(1)}) custom-call(bf16[2,4,64,64,126]{4,3,2,1,0:T(8,128)(2,1)} %bitcast.7, bf16[32,32,128]{2,1,0:T(8,128)(2,1)S(1)} %get-tuple-element.25.leaf_ref.own_ref, bf16[32,32,128]{2,1,0:T(8,128)(2,1)S(1)} %collective-permute-done.near_ref, ...), custom_call_target="tpu_custom_call" | custom-call | tf_op jit(solution)/shard_map/pallas_call | solution.py:229
  17.3 0.2 collective-permute-start.5
  17.5 2.4 %collective-permute-done.6.next_ref = bf16[31,32,128]{2,1,0:T(8,128)(2,1)} collective-permute-done((bf16[31,32,128]{2,1,0:T(8,128)(2,1)S(1)}, bf16[31,32,128]{2,1,0:T(8,128)(2,1)}, u32[]{:S(2)}, u32[]{:S(2)}) %collective-permute-start.6) | collective-permute-done | bytes 253984 | tf_op jit(solution)/shard_map/ppermute | solution.py:376
  19.9 0.6 %collective-permute-done.2.near_ref = bf16[31,32,128]{2,1,0:T(8,128)(2,1)S(1)} collective-permute-done((bf16[31,32,128]{2,1,0:T(8,128)(2,1)S(1)}, bf16[31,32,128]{2,1,0:T(8,128)(2,1)S(1)}, u32[]{:S(2)}, u32[]{:S(2)}) %collective-permute-start.2) | collective-permute-done | bytes 253984 | tf_op jit(solution)/shard_map/ppermute | solution.py:376
  20.5 1.3 %shard_map.50 = (bf16[2,218,32,128]{3,2,1,0:T(8,128)(2,1)S(1)}, bf16[93,32,128]{2,1,0:T(8,128)(2,1)S(1)}) custom-call(bf16[31,32,128]{2,1,0:T(8,128)(2,1)S(1)} %get-tuple-element.37.own_ref, bf16[31,32,128]{2,1,0:T(8,128)(2,1)S(1)} %collective-permute-done.2.near_ref, bf16[31,32,128]{2,1,0:T(8,128)(2,1)} %collective-permute-done.6.next_ref), custom_call_target="tpu_custom_call" | custom-call | tf_op jit(solution)/shard_map/pallas_call | solution.py:244
  21.8 0.1 collective-permute-start.7
  21.9 0.1 collective-permute-start.4
  22.0 0.3 collective-permute-start.3
  22.2 1.9 %collective-permute-done.7.upper_ref = bf16[93,32,128]{2,1,0:T(8,128)(2,1)S(1)} collective-permute-done((bf16[93,32,128]{2,1,0:T(8,128)(2,1)S(1)}, bf16[93,32,128]{2,1,0:T(8,128)(2,1)S(1)}, u32[]{:S(2)}, u32[]{:S(2)}) %collective-permute-start.7) | collective-permute-done | bytes 761888 | tf_op jit(solution)/shard_map/ppermute | solution.py:376
  24.1 0.0 collective-permute-done.5.leaf_ref
  24.1 0.6 %shard_map.51 = (bf16[2,225,32,128]{3,2,1,0:T(8,128)(2,1)S(1)}, bf16[2,218,32,128]{3,2,1,0:T(8,128)(2,1)S(1)}) custom-call(bf16[96,32,128]{2,1,0:T(8,128)(2,1)S(1)} %collective-permute-done.5.leaf_ref, bf16[93,32,128]{2,1,0:T(8,128)(2,1)S(1)} %collective-permute-done.7.upper_ref, ...), custom_call_target="tpu_custom_call", output_to_operand_aliasing={{0}: (2, {}), {1}: (3, {})} | custom-call | tf_op jit(solution)/shard_map/pallas_call | solution.py:260
  24.7 6.9 %collective-permute-done.4.far_ref = bf16[32,32,128]{2,1,0:T(8,128)(2,1)S(1)} collective-permute-done((bf16[32,32,128]{2,1,0:T(8,128)(2,1)S(1)}, bf16[32,32,128]{2,1,0:T(8,128)(2,1)S(1)}, u32[]{:S(2)}, u32[]{:S(2)}) %collective-permute-start.4) | collective-permute-done | bytes 262176 | tf_op jit(solution)/shard_map/ppermute | solution.py:376
  31.7 2.2 %shard_map.52 = (f32[32,32,128]{2,1,0:T(8,128)S(1)}, bf16[2,225,32,128]{3,2,1,0:T(8,128)(2,1)S(1)}) custom-call(s32[8,126]{1,0:T(8,128)S(1)} %get-tuple-element.30.place_ref, bf16[32,32,128]{2,1,0:T(8,128)(2,1)S(1)} %collective-permute-done.4.far_ref, bf16[126,128,128]{2,1,0:T(8,128)(2,1)S(1)} %get-tuple-element.31.first_ref, ...), custom_call_target="tpu_custom_call", output_to_operand_aliasing={{1}: (4, {})} | custom-call | tf_op jit(solution)/shard_map/pallas_call | solution.py:306
  33.8 0.6 %collective-permute-done.3.far_ref = bf16[31,32,128]{2,1,0:T(8,128)(2,1)S(1)} collective-permute-done((bf16[31,32,128]{2,1,0:T(8,128)(2,1)S(1)}, bf16[31,32,128]{2,1,0:T(8,128)(2,1)S(1)}, u32[]{:S(2)}, u32[]{:S(2)}) %collective-permute-start.3) | collective-permute-done | bytes 253984 | tf_op jit(solution)/shard_map/ppermute | solution.py:376
  34.4 3.8 %shard_map.53 = (f32[64,32,64]{2,1,0:T(8,128)}, bf16[2,218,32,128]{3,2,1,0:T(8,128)(2,1)S(1)}) custom-call(s32[8,126]{1,0:T(8,128)S(1)} %get-tuple-element.30.place_ref, bf16[31,32,128]{2,1,0:T(8,128)(2,1)S(1)} %collective-permute-done.3.far_ref, bf16[126,128,128]{2,1,0:T(8,128)(2,1)S(1)} %get-tuple-element.31.first_ref, ...), custom_call_target="tpu_custom_call", output_to_operand_aliasing={{1}: (6, {})} | custom-call | tf_op jit(solution)/shard_map/pallas_call | solution.py:353
Async XLA Ops:
  1.4 11.6 %collective-permute-start.1 = (bf16[32,32,128]{2,1,0:T(8,128)(2,1)S(1)}, bf16[32,32,128]{2,1,0:T(8,128)(2,1)S(1)}, u32[]{:S(2)}, u32[]{:S(2)}) collective-permute-start(bf16[32,32,128]{2,1,0:T(8,128)(2,1)S(1)} %get-tuple-element.25.leaf_ref.own_ref), channel_id=1, source_target_pairs={{0,16},{8,248},{16,32},{24,8},{32,48},{40,24},{48,64},{56,40},{64,... | collective-permute-start | bytes 786440 | tf_op jit(solution)/shard_map/ppermute | solution.py:376
  3.1 10.9 %collective-permute-start = (bf16[32,32,128]{2,1,0:T(8,128)(2,1)S(1)}, bf16[32,32,128]{2,1,0:T(8,128)(2,1)S(1)}, u32[]{:S(2)}, u32[]{:S(2)}) collective-permute-start(bf16[32,32,128]{2,1,0:T(8,128)(2,1)S(1)} %get-tuple-element.25.leaf_ref.own_ref), channel_id=1, source_target_pairs={{0,248},{8,16},{16,8},{24,32},{32,24},{40,48},{48,40},{56,64},{64,... | collective-permute-start | bytes 786440 | tf_op jit(solution)/shard_map/ppermute | solution.py:376
  8.1 11.8 %collective-permute-start.6 = (bf16[31,32,128]{2,1,0:T(8,128)(2,1)S(1)}, bf16[31,32,128]{2,1,0:T(8,128)(2,1)}, u32[]{:S(2)}, u32[]{:S(2)}) collective-permute-start(bf16[31,32,128]{2,1,0:T(8,128)(2,1)S(1)} %get-tuple-element.37.own_ref), channel_id=1, source_target_pairs={{0,16},{8,248},{16,32},{24,8},{32,48},{40,24},{48,64},{56,40},{64,... | collective-permute-start | bytes 761864 | tf_op jit(solution)/shard_map/ppermute | solution.py:376
  9.4 11.0 %collective-permute-start.2 = (bf16[31,32,128]{2,1,0:T(8,128)(2,1)S(1)}, bf16[31,32,128]{2,1,0:T(8,128)(2,1)S(1)}, u32[]{:S(2)}, u32[]{:S(2)}) collective-permute-start(bf16[31,32,128]{2,1,0:T(8,128)(2,1)S(1)} %get-tuple-element.37.own_ref), channel_id=1, source_target_pairs={{0,248},{8,16},{16,8},{24,32},{32,24},{40,48},{48,40},{56,64},{64,... | collective-permute-start | bytes 761864 | tf_op jit(solution)/shard_map/ppermute | solution.py:376
  17.3 6.9 %collective-permute-start.5 = (bf16[96,32,128]{2,1,0:T(8,128)(2,1)S(1)}, bf16[96,32,128]{2,1,0:T(8,128)(2,1)S(1)}, u32[]{:S(2)}, u32[]{:S(2)}) collective-permute-start(bf16[96,32,128]{2,1,0:T(8,128)(2,1)S(1)} %get-tuple-element.36), channel_id=1, source_target_pairs={{0,8},{8,0},{16,24},{24,16},{32,40},{40,32},{48,56},{56,48},{64,72... | collective-permute-start | bytes 2359304 | tf_op jit(solution)/shard_map/ppermute | solution.py:376
  21.8 2.3 %collective-permute-start.7 = (bf16[93,32,128]{2,1,0:T(8,128)(2,1)S(1)}, bf16[93,32,128]{2,1,0:T(8,128)(2,1)S(1)}, u32[]{:S(2)}, u32[]{:S(2)}) collective-permute-start(bf16[93,32,128]{2,1,0:T(8,128)(2,1)S(1)} %get-tuple-element.38), channel_id=1, source_target_pairs={{0,8},{8,0},{16,24},{24,16},{32,40},{40,32},{48,56},{56,48},{64,72... | collective-permute-start | bytes 2285576 | tf_op jit(solution)/shard_map/ppermute | solution.py:376
  21.9 9.8 %collective-permute-start.4 = (bf16[32,32,128]{2,1,0:T(8,128)(2,1)S(1)}, bf16[32,32,128]{2,1,0:T(8,128)(2,1)S(1)}, u32[]{:S(2)}, u32[]{:S(2)}) collective-permute-start(bf16[32,32,128]{2,1,0:T(8,128)(2,1)S(1)} %collective-permute-done.near_ref), channel_id=1, source_target_pairs={{0,16},{8,248},{16,32},{24,8},{32,48},{40,24},{48,64},{56,40},{64,... | collective-permute-start | bytes 786440 | tf_op jit(solution)/shard_map/ppermute | solution.py:376
  22.0 12.4 %collective-permute-start.3 = (bf16[31,32,128]{2,1,0:T(8,128)(2,1)S(1)}, bf16[31,32,128]{2,1,0:T(8,128)(2,1)S(1)}, u32[]{:S(2)}, u32[]{:S(2)}) collective-permute-start(bf16[31,32,128]{2,1,0:T(8,128)(2,1)S(1)} %collective-permute-done.2.near_ref), channel_id=1, source_target_pairs={{0,16},{8,248},{16,32},{24,8},{32,48},{40,24},{48,64},{56,40},{64,... | collective-permute-start | bytes 761864 | tf_op jit(solution)/shard_map/ppermute | solution.py:376

commit v5 on v4

--- a/solution.py
+++ b/solution.py
@@ -218,9 +218,22 @@
     )
 
 
-def second_weights_kernel(tiles_ref, own_ref, near_ref, next_ref, out_ref, table_ref, sent_ref, held, stage, sem):
+def second_weights_kernel(
+    tiles_ref, own_ref, near_ref, next_ref, out_ref, table_ref, sent_ref, held, stage, sem, next_sem
+):
+    last = sent_ref.at[pl.ds(2 * LEAF_PAIRS, LEAF_PAIRS)]
+    next_copy = pltpu.make_async_copy(next_ref, last, next_sem)
+    next_copy.start()
+
     def beside():
-        fill_first(own_ref, near_ref, next_ref, table_ref, sent_ref, LEAF_PAIRS)
+        for place, (number, block) in enumerate(((REACH, own_ref), (REACH - 1, near_ref))):
+            fill_block(table_ref, block, number, LEAF_PAIRS)
+            for i in range(LEAF_PAIRS):
+                sent_ref[place * LEAF_PAIRS + i] = block[i]
+        for half in range(2):
+            table_ref[half, 7 * LEAF_PAIRS] = jnp.zeros((ROWS, LANES), BF16)
+        next_copy.wait()
+        fill_block(table_ref, sent_ref, REACH - 2, LEAF_PAIRS, 2 * LEAF_PAIRS)
 
     transpose_tiles(1, tiles_ref, out_ref, held, stage, sem, beside)
 
@@ -228,12 +241,12 @@
 def second_weights(slabs, own, near, next_near):
     return pl.pallas_call(
         second_weights_kernel,
-        in_specs=[IN_HBM, WHOLE, WHOLE, WHOLE],
+        in_specs=[IN_HBM, WHOLE, WHOLE, IN_HBM],
         out_specs=(WHOLE, WHOLE, WHOLE),
         out_shape=(pltpu.VMEM((NODES, 2 * K, LANES), BF16), *table_and_sent(LEAF_PAIRS)),
-        scratch_shapes=TRANSPOSE_SCRATCH,
+        scratch_shapes=[*TRANSPOSE_SCRATCH, pltpu.SemaphoreType.DMA],
         compiler_params=params(12),
-    )(in_hbm(slabs), *in_vmem(own, near, next_near))
+    )(in_hbm(slabs), *in_vmem(own, near), in_hbm(next_near))
 
 
 def upper_table_kernel(own_ref, near_ref, next_ref, table_ref, sent_ref):

time: 38.5 us -> 37.5 us (0.974)
  Pallas kernels: 17.3 us -> 16.5 us
    pallas_call x1, Pallas kernels: 1.32 us -> 0.33 us  [upper_table(): pl.pallas_call(upper_table_kernel, in_specs=[WHOLE, WHOLE, WHOLE], out_sp...]
  transfers between devices with their start and end apart: 8 -> 8, of which waited for: 6 -> 7; matrix products, arithmetic and copies ran while one was open for 0% -> 0% of each run, Pallas kernels for 31% -> 30%
where the time goes in v5:
time: 37.5 us; the launch traced here: 37.4 us
  Pallas kernels  16.5 us (44%)
  waiting for transfers between devices  13.1 us (35%)
  starting transfers between devices  7.55 us (20%)
    ppermute x8, waiting for transfers between devices, moved(): lax.ppermute(block, 'clus', [(i, target(i) % count) for i in range(count)])  13.1 us
    ppermute x8, starting transfers between devices, moved(): lax.ppermute(block, 'clus', [(i, target(i) % count) for i in range(count)])  7.55 us
    pallas_call x1, Pallas kernels, upper_levels(): pl.pallas_call(upper_kernel, in_specs=[IN_SMEM] + [WHOLE] * 6, out_specs=...  3.81 us
    pallas_call x1, Pallas kernels, second_weights(): pl.pallas_call(second_weights_kernel, in_specs=[IN_HBM, WHOLE, WHOLE, IN_...  3.46 us
    pallas_call x1, Pallas kernels, first_weights(): pl.pallas_call(first_weights_kernel, in_specs=[IN_HBM, IN_HBM, IN_SMEM],...  3.19 us
    pallas_call x1, Pallas kernels, leaf_level(): pl.pallas_call(leaf_kernel, in_specs=[IN_SMEM] + [WHOLE] * 4, out_specs=(...  2.16 us
    pallas_call x1, Pallas kernels, upward(): pl.pallas_call(upward_kernel, in_specs=[WHOLE, WHOLE], out_specs=(WHOLE,...  1.52 us
    pallas_call x1, Pallas kernels, front(): pl.pallas_call(front_kernel, in_specs=[IN_HBM, IN_HBM], out_specs=(WHOLE,...  1.4 us
  transfers between devices with their start and end apart: 8, of which 7 were waited for; matrix products, arithmetic and copies ran while one was open for 0% of the time, Pallas kernels for 30%

profile of v5, /device:TPU:128, one launch (start us, length us, event | category | flops | bytes accessed | tf_op | source)
XLA Modules:
  0.0 37.4 jit_solution(673668361086424788)
XLA Ops:
  0.0 1.4 %shard_map.46 = (bf16[32,32,128]{2,1,0:T(8,128)(2,1)S(1)}, bf16[64,64,124]{2,1,0:T(8,128)(2,1)S(1)}) custom-call(bf16[64,32,64]{2,1,0:T(8,128)(2,1)} %leaf_ref.1, bf16[64,64,124]{2,1,0:T(8,128)(2,1)} %bitcast.8), custom_call_target="tpu_custom_call" | custom-call | tf_op jit(solution)/shard_map/pallas_call | solution.py:67
  1.4 1.7 %collective-permute-start.1 = (bf16[32,32,128]{2,1,0:T(8,128)(2,1)S(1)}, bf16[32,32,128]{2,1,0:T(8,128)(2,1)}, u32[]{:S(2)}, u32[]{:S(2)}) collective-permute-start(bf16[32,32,128]{2,1,0:T(8,128)(2,1)S(1)} %get-tuple-element.25.leaf_ref.own_ref), channel_id=1, source_target_pairs={{0,16},{8,248},{16,32},{24,8},{32,48},{40,24},{48,64},{56,40},{64,... | collective-permute-start | bytes 786440 | tf_op jit(solution)/shard_map/ppermute | solution.py:389
  3.1 3.5 %collective-permute-start = (bf16[32,32,128]{2,1,0:T(8,128)(2,1)S(1)}, bf16[32,32,128]{2,1,0:T(8,128)(2,1)S(1)}, u32[]{:S(2)}, u32[]{:S(2)}) collective-permute-start(bf16[32,32,128]{2,1,0:T(8,128)(2,1)S(1)} %get-tuple-element.25.leaf_ref.own_ref), channel_id=1, source_target_pairs={{0,248},{8,16},{16,8},{24,32},{32,24},{40,48},{48,40},{56,64},{64,... | collective-permute-start | bytes 786440 | tf_op jit(solution)/shard_map/ppermute | solution.py:389
  6.6 1.5 %shard_map.47 = (bf16[31,256,128]{2,1,0:T(8,128)(2,1)S(1)}, bf16[31,32,128]{2,1,0:T(8,128)(2,1)S(1)}) custom-call(bf16[64,64,124]{2,1,0:T(8,128)(2,1)S(1)} %get-tuple-element.26.coeff_ref, bf16[32,32,128]{2,1,0:T(8,128)(2,1)S(1)} %get-tuple-element.25.leaf_ref.own_ref), custom_call_target="tpu_custom_call" | custom-call | tf_op jit(solution)/shard_map/pallas_call | solution.py:105
  8.1 1.3 %collective-permute-start.6 = (bf16[31,32,128]{2,1,0:T(8,128)(2,1)S(1)}, bf16[31,32,128]{2,1,0:T(8,128)(2,1)S(1)}, u32[]{:S(2)}, u32[]{:S(2)}) collective-permute-start(bf16[31,32,128]{2,1,0:T(8,128)(2,1)S(1)} %get-tuple-element.37.own_ref), channel_id=1, source_target_pairs={{0,16},{8,248},{16,32},{24,8},{32,48},{40,24},{48,64},{56,40},{64,... | collective-permute-start | bytes 761864 | tf_op jit(solution)/shard_map/ppermute | solution.py:389
  9.4 0.4 %collective-permute-start.2 = (bf16[31,32,128]{2,1,0:T(8,128)(2,1)S(1)}, bf16[31,32,128]{2,1,0:T(8,128)(2,1)S(1)}, u32[]{:S(2)}, u32[]{:S(2)}) collective-permute-start(bf16[31,32,128]{2,1,0:T(8,128)(2,1)S(1)} %get-tuple-element.37.own_ref), channel_id=1, source_target_pairs={{0,248},{8,16},{16,8},{24,32},{32,24},{40,48},{48,40},{56,64},{64,... | collective-permute-start | bytes 761864 | tf_op jit(solution)/shard_map/ppermute | solution.py:389
  9.8 3.2 %shard_map.48 = (bf16[126,128,128]{2,1,0:T(8,128)(2,1)S(1)}, s32[8,126]{1,0:T(8,128)S(1)}) custom-call(bf16[2,4,64,64,126]{4,3,2,1,0:T(8,128)(2,1)} %bitcast.6, s32[8,126]{1,0:T(8,128)} %bitcast.9, s32[1]{0:T(128)} %bitcast.4.device_ref), custom_call_target="tpu_custom_call" | custom-call | tf_op jit(solution)/shard_map/pallas_call | solution.py:181
  13.0 0.1 collective-permute-done.1.next_ref
  13.1 0.9 %collective-permute-done.near_ref = bf16[32,32,128]{2,1,0:T(8,128)(2,1)S(1)} collective-permute-done((bf16[32,32,128]{2,1,0:T(8,128)(2,1)S(1)}, bf16[32,32,128]{2,1,0:T(8,128)(2,1)S(1)}, u32[]{:S(2)}, u32[]{:S(2)}) %collective-permute-start) | collective-permute-done | bytes 262176 | tf_op jit(solution)/shard_map/ppermute | solution.py:389
  14.0 3.5 %shard_map.49 = (bf16[126,128,128]{2,1,0:T(8,128)(2,1)S(1)}, bf16[2,225,32,128]{3,2,1,0:T(8,128)(2,1)S(1)}, bf16[96,32,128]{2,1,0:T(8,128)(2,1)S(1)}) custom-call(bf16[2,4,64,64,126]{4,3,2,1,0:T(8,128)(2,1)} %bitcast.7, bf16[32,32,128]{2,1,0:T(8,128)(2,1)S(1)} %get-tuple-element.25.leaf_ref.own_ref, bf16[32,32,128]{2,1,0:T(8,128)(2,1)S(1)} %collective-permute-done.near_ref, ...), custom_call_target="tpu_custom_call" | custom-call | tf_op jit(solution)/shard_map/pallas_call | solution.py:242
  17.5 0.2 collective-permute-start.5
  17.7 2.1 %collective-permute-done.6.next_ref = bf16[31,32,128]{2,1,0:T(8,128)(2,1)S(1)} collective-permute-done((bf16[31,32,128]{2,1,0:T(8,128)(2,1)S(1)}, bf16[31,32,128]{2,1,0:T(8,128)(2,1)S(1)}, u32[]{:S(2)}, u32[]{:S(2)}) %collective-permute-start.6) | collective-permute-done | bytes 253984 | tf_op jit(solution)/shard_map/ppermute | solution.py:389
  19.8 0.7 %collective-permute-done.2.near_ref = bf16[31,32,128]{2,1,0:T(8,128)(2,1)S(1)} collective-permute-done((bf16[31,32,128]{2,1,0:T(8,128)(2,1)S(1)}, bf16[31,32,128]{2,1,0:T(8,128)(2,1)S(1)}, u32[]{:S(2)}, u32[]{:S(2)}) %collective-permute-start.2) | collective-permute-done | bytes 253984 | tf_op jit(solution)/shard_map/ppermute | solution.py:389
  20.5 0.3 shard_map.50
  20.8 0.1 collective-permute-start.7
  20.9 0.1 collective-permute-start.4
  21.0 0.3 collective-permute-start.3
  21.3 1.9 %collective-permute-done.7.upper_ref = bf16[93,32,128]{2,1,0:T(8,128)(2,1)S(1)} collective-permute-done((bf16[93,32,128]{2,1,0:T(8,128)(2,1)S(1)}, bf16[93,32,128]{2,1,0:T(8,128)(2,1)S(1)}, u32[]{:S(2)}, u32[]{:S(2)}) %collective-permute-start.7) | collective-permute-done | bytes 761888 | tf_op jit(solution)/shard_map/ppermute | solution.py:389
  23.1 0.0 collective-permute-done.5.leaf_ref
  23.1 0.6 %shard_map.51 = (bf16[2,225,32,128]{3,2,1,0:T(8,128)(2,1)S(1)}, bf16[2,218,32,128]{3,2,1,0:T(8,128)(2,1)S(1)}) custom-call(bf16[96,32,128]{2,1,0:T(8,128)(2,1)S(1)} %collective-permute-done.5.leaf_ref, bf16[93,32,128]{2,1,0:T(8,128)(2,1)S(1)} %collective-permute-done.7.upper_ref, ...), custom_call_target="tpu_custom_call", output_to_operand_aliasing={{0}: (2, {}), {1}: (3, {})} | custom-call | tf_op jit(solution)/shard_map/pallas_call | solution.py:273
  23.7 6.9 %collective-permute-done.4.far_ref = bf16[32,32,128]{2,1,0:T(8,128)(2,1)S(1)} collective-permute-done((bf16[32,32,128]{2,1,0:T(8,128)(2,1)S(1)}, bf16[32,32,128]{2,1,0:T(8,128)(2,1)S(1)}, u32[]{:S(2)}, u32[]{:S(2)}) %collective-permute-start.4) | collective-permute-done | bytes 262176 | tf_op jit(solution)/shard_map/ppermute | solution.py:389
  30.7 2.2 %shard_map.52 = (f32[32,32,128]{2,1,0:T(8,128)S(1)}, bf16[2,225,32,128]{3,2,1,0:T(8,128)(2,1)S(1)}) custom-call(s32[8,126]{1,0:T(8,128)S(1)} %get-tuple-element.30.place_ref, bf16[32,32,128]{2,1,0:T(8,128)(2,1)S(1)} %collective-permute-done.4.far_ref, bf16[126,128,128]{2,1,0:T(8,128)(2,1)S(1)} %get-tuple-element.31.first_ref, ...), custom_call_target="tpu_custom_call", output_to_operand_aliasing={{1}: (4, {})} | custom-call | tf_op jit(solution)/shard_map/pallas_call | solution.py:319
  32.8 0.6 %collective-permute-done.3.far_ref = bf16[31,32,128]{2,1,0:T(8,128)(2,1)S(1)} collective-permute-done((bf16[31,32,128]{2,1,0:T(8,128)(2,1)S(1)}, bf16[31,32,128]{2,1,0:T(8,128)(2,1)S(1)}, u32[]{:S(2)}, u32[]{:S(2)}) %collective-permute-start.3) | collective-permute-done | bytes 253984 | tf_op jit(solution)/shard_map/ppermute | solution.py:389
  33.4 3.8 %shard_map.53 = (f32[64,32,64]{2,1,0:T(8,128)}, bf16[2,218,32,128]{3,2,1,0:T(8,128)(2,1)S(1)}) custom-call(s32[8,126]{1,0:T(8,128)S(1)} %get-tuple-element.30.place_ref, bf16[31,32,128]{2,1,0:T(8,128)(2,1)S(1)} %collective-permute-done.3.far_ref, bf16[126,128,128]{2,1,0:T(8,128)(2,1)S(1)} %get-tuple-element.31.first_ref, ...), custom_call_target="tpu_custom_call", output_to_operand_aliasing={{1}: (6, {})} | custom-call | tf_op jit(solution)/shard_map/pallas_call | solution.py:366
Async XLA Ops:
  1.4 11.7 %collective-permute-start.1 = (bf16[32,32,128]{2,1,0:T(8,128)(2,1)S(1)}, bf16[32,32,128]{2,1,0:T(8,128)(2,1)}, u32[]{:S(2)}, u32[]{:S(2)}) collective-permute-start(bf16[32,32,128]{2,1,0:T(8,128)(2,1)S(1)} %get-tuple-element.25.leaf_ref.own_ref), channel_id=1, source_target_pairs={{0,16},{8,248},{16,32},{24,8},{32,48},{40,24},{48,64},{56,40},{64,... | collective-permute-start | bytes 786440 | tf_op jit(solution)/shard_map/ppermute | solution.py:389
  3.1 10.9 %collective-permute-start = (bf16[32,32,128]{2,1,0:T(8,128)(2,1)S(1)}, bf16[32,32,128]{2,1,0:T(8,128)(2,1)S(1)}, u32[]{:S(2)}, u32[]{:S(2)}) collective-permute-start(bf16[32,32,128]{2,1,0:T(8,128)(2,1)S(1)} %get-tuple-element.25.leaf_ref.own_ref), channel_id=1, source_target_pairs={{0,248},{8,16},{16,8},{24,32},{32,24},{40,48},{48,40},{56,64},{64,... | collective-permute-start | bytes 786440 | tf_op jit(solution)/shard_map/ppermute | solution.py:389
  8.1 11.7 %collective-permute-start.6 = (bf16[31,32,128]{2,1,0:T(8,128)(2,1)S(1)}, bf16[31,32,128]{2,1,0:T(8,128)(2,1)S(1)}, u32[]{:S(2)}, u32[]{:S(2)}) collective-permute-start(bf16[31,32,128]{2,1,0:T(8,128)(2,1)S(1)} %get-tuple-element.37.own_ref), channel_id=1, source_target_pairs={{0,16},{8,248},{16,32},{24,8},{32,48},{40,24},{48,64},{56,40},{64,... | collective-permute-start | bytes 761864 | tf_op jit(solution)/shard_map/ppermute | solution.py:389
  9.4 11.0 %collective-permute-start.2 = (bf16[31,32,128]{2,1,0:T(8,128)(2,1)S(1)}, bf16[31,32,128]{2,1,0:T(8,128)(2,1)S(1)}, u32[]{:S(2)}, u32[]{:S(2)}) collective-permute-start(bf16[31,32,128]{2,1,0:T(8,128)(2,1)S(1)} %get-tuple-element.37.own_ref), channel_id=1, source_target_pairs={{0,248},{8,16},{16,8},{24,32},{32,24},{40,48},{48,40},{56,64},{64,... | collective-permute-start | bytes 761864 | tf_op jit(solution)/shard_map/ppermute | solution.py:389
  17.5 5.7 %collective-permute-start.5 = (bf16[96,32,128]{2,1,0:T(8,128)(2,1)S(1)}, bf16[96,32,128]{2,1,0:T(8,128)(2,1)S(1)}, u32[]{:S(2)}, u32[]{:S(2)}) collective-permute-start(bf16[96,32,128]{2,1,0:T(8,128)(2,1)S(1)} %get-tuple-element.36), channel_id=1, source_target_pairs={{0,8},{8,0},{16,24},{24,16},{32,40},{40,32},{48,56},{56,48},{64,72... | collective-permute-start | bytes 2359304 | tf_op jit(solution)/shard_map/ppermute | solution.py:389
  20.8 2.3 %collective-permute-start.7 = (bf16[93,32,128]{2,1,0:T(8,128)(2,1)S(1)}, bf16[93,32,128]{2,1,0:T(8,128)(2,1)S(1)}, u32[]{:S(2)}, u32[]{:S(2)}) collective-permute-start(bf16[93,32,128]{2,1,0:T(8,128)(2,1)S(1)} %get-tuple-element.38), channel_id=1, source_target_pairs={{0,8},{8,0},{16,24},{24,16},{32,40},{40,32},{48,56},{56,48},{64,72... | collective-permute-start | bytes 2285576 | tf_op jit(solution)/shard_map/ppermute | solution.py:389
  20.9 9.8 %collective-permute-start.4 = (bf16[32,32,128]{2,1,0:T(8,128)(2,1)S(1)}, bf16[32,32,128]{2,1,0:T(8,128)(2,1)S(1)}, u32[]{:S(2)}, u32[]{:S(2)}) collective-permute-start(bf16[32,32,128]{2,1,0:T(8,128)(2,1)S(1)} %collective-permute-done.near_ref), channel_id=1, source_target_pairs={{0,16},{8,248},{16,32},{24,8},{32,48},{40,24},{48,64},{56,40},{64,... | collective-permute-start | bytes 786440 | tf_op jit(solution)/shard_map/ppermute | solution.py:389
  21.0 12.4 %collective-permute-start.3 = (bf16[31,32,128]{2,1,0:T(8,128)(2,1)S(1)}, bf16[31,32,128]{2,1,0:T(8,128)(2,1)S(1)}, u32[]{:S(2)}, u32[]{:S(2)}) collective-permute-start(bf16[31,32,128]{2,1,0:T(8,128)(2,1)S(1)} %collective-permute-done.2.near_ref), channel_id=1, source_target_pairs={{0,16},{8,248},{16,32},{24,8},{32,48},{40,24},{48,64},{56,40},{64,... | collective-permute-start | bytes 761864 | tf_op jit(solution)/shard_map/ppermute | solution.py:389

commit v6 on v5

--- a/solution.py
+++ b/solution.py
@@ -110,7 +110,7 @@
             pltpu.VMEM((UPPER_PAIRS, 4 * K, LANES), BF16),
             pltpu.VMEM((UPPER_PAIRS, ROWS, LANES), BF16),
         ),
-        scratch_shapes=[pltpu.VMEM((E_NODES * E_STRIDE + 8, LANES), F32)],
+        scratch_shapes=[pltpu.VMEM((LANES * E_STRIDE + 8, LANES), F32)],
         compiler_params=params(14),
     )(*in_vmem(coeffs, leaf_pairs))
 
@@ -165,7 +165,7 @@
 
 TRANSPOSE_SCRATCH = [
     pltpu.VMEM((2, 2, K, K, NODES), BF16),
-    pltpu.VMEM((NODES * STRIDE + 8, LANES), F32),
+    pltpu.VMEM((LANES * STRIDE + 8, LANES), F32),
     pltpu.SemaphoreType.DMA((CHUNKS,)),
 ]
 

time: 37.5 us -> 37.5 us (level)
  no operation moved by 1% of the time
where the time goes in v6:
time: 37.5 us; the launch traced here: 37.4 us
  Pallas kernels  16.5 us (44%)
  waiting for transfers between devices  13.1 us (35%)
  starting transfers between devices  7.55 us (20%)
    ppermute x8, waiting for transfers between devices, moved(): lax.ppermute(block, 'clus', [(i, target(i) % count) for i in range(count)])  13.1 us
    ppermute x8, starting transfers between devices, moved(): lax.ppermute(block, 'clus', [(i, target(i) % count) for i in range(count)])  7.55 us
    pallas_call x1, Pallas kernels, upper_levels(): pl.pallas_call(upper_kernel, in_specs=[IN_SMEM] + [WHOLE] * 6, out_specs=...  3.81 us
    pallas_call x1, Pallas kernels, second_weights(): pl.pallas_call(second_weights_kernel, in_specs=[IN_HBM, WHOLE, WHOLE, IN_...  3.46 us
    pallas_call x1, Pallas kernels, first_weights(): pl.pallas_call(first_weights_kernel, in_specs=[IN_HBM, IN_HBM, IN_SMEM],...  3.19 us
    pallas_call x1, Pallas kernels, leaf_level(): pl.pallas_call(leaf_kernel, in_specs=[IN_SMEM] + [WHOLE] * 4, out_specs=(...  2.16 us
    pallas_call x1, Pallas kernels, upward(): pl.pallas_call(upward_kernel, in_specs=[WHOLE, WHOLE], out_specs=(WHOLE,...  1.52 us
    pallas_call x1, Pallas kernels, front(): pl.pallas_call(front_kernel, in_specs=[IN_HBM, IN_HBM], out_specs=(WHOLE,...  1.4 us
  transfers between devices with their start and end apart: 8, of which 7 were waited for; matrix products, arithmetic and copies ran while one was open for 0% of the time, Pallas kernels for 30%

profile of v6, /device:TPU:128, one launch (start us, length us, event | category | flops | bytes accessed | tf_op | source)
XLA Modules:
  0.0 37.4 jit_solution(12415238519533898510)
XLA Ops:
  0.0 1.4 %shard_map.46 = (bf16[32,32,128]{2,1,0:T(8,128)(2,1)S(1)}, bf16[64,64,124]{2,1,0:T(8,128)(2,1)S(1)}) custom-call(bf16[64,32,64]{2,1,0:T(8,128)(2,1)} %leaf_ref.1, bf16[64,64,124]{2,1,0:T(8,128)(2,1)} %bitcast.8), custom_call_target="tpu_custom_call" | custom-call | tf_op jit(solution)/shard_map/pallas_call | solution.py:67
  1.4 1.7 %collective-permute-start.1 = (bf16[32,32,128]{2,1,0:T(8,128)(2,1)S(1)}, bf16[32,32,128]{2,1,0:T(8,128)(2,1)}, u32[]{:S(2)}, u32[]{:S(2)}) collective-permute-start(bf16[32,32,128]{2,1,0:T(8,128)(2,1)S(1)} %get-tuple-element.25.leaf_ref.own_ref), channel_id=1, source_target_pairs={{0,16},{8,248},{16,32},{24,8},{32,48},{40,24},{48,64},{56,40},{64,... | collective-permute-start | bytes 786440 | tf_op jit(solution)/shard_map/ppermute | solution.py:389
  3.1 3.5 %collective-permute-start = (bf16[32,32,128]{2,1,0:T(8,128)(2,1)S(1)}, bf16[32,32,128]{2,1,0:T(8,128)(2,1)S(1)}, u32[]{:S(2)}, u32[]{:S(2)}) collective-permute-start(bf16[32,32,128]{2,1,0:T(8,128)(2,1)S(1)} %get-tuple-element.25.leaf_ref.own_ref), channel_id=1, source_target_pairs={{0,248},{8,16},{16,8},{24,32},{32,24},{40,48},{48,40},{56,64},{64,... | collective-permute-start | bytes 786440 | tf_op jit(solution)/shard_map/ppermute | solution.py:389
  6.6 1.5 %shard_map.47 = (bf16[31,256,128]{2,1,0:T(8,128)(2,1)S(1)}, bf16[31,32,128]{2,1,0:T(8,128)(2,1)S(1)}) custom-call(bf16[64,64,124]{2,1,0:T(8,128)(2,1)S(1)} %get-tuple-element.26.coeff_ref, bf16[32,32,128]{2,1,0:T(8,128)(2,1)S(1)} %get-tuple-element.25.leaf_ref.own_ref), custom_call_target="tpu_custom_call" | custom-call | tf_op jit(solution)/shard_map/pallas_call | solution.py:105
  8.1 1.3 %collective-permute-start.6 = (bf16[31,32,128]{2,1,0:T(8,128)(2,1)S(1)}, bf16[31,32,128]{2,1,0:T(8,128)(2,1)S(1)}, u32[]{:S(2)}, u32[]{:S(2)}) collective-permute-start(bf16[31,32,128]{2,1,0:T(8,128)(2,1)S(1)} %get-tuple-element.37.own_ref), channel_id=1, source_target_pairs={{0,16},{8,248},{16,32},{24,8},{32,48},{40,24},{48,64},{56,40},{64,... | collective-permute-start | bytes 761864 | tf_op jit(solution)/shard_map/ppermute | solution.py:389
  9.4 0.4 %collective-permute-start.2 = (bf16[31,32,128]{2,1,0:T(8,128)(2,1)S(1)}, bf16[31,32,128]{2,1,0:T(8,128)(2,1)S(1)}, u32[]{:S(2)}, u32[]{:S(2)}) collective-permute-start(bf16[31,32,128]{2,1,0:T(8,128)(2,1)S(1)} %get-tuple-element.37.own_ref), channel_id=1, source_target_pairs={{0,248},{8,16},{16,8},{24,32},{32,24},{40,48},{48,40},{56,64},{64,... | collective-permute-start | bytes 761864 | tf_op jit(solution)/shard_map/ppermute | solution.py:389
  9.8 3.2 %shard_map.48 = (bf16[126,128,128]{2,1,0:T(8,128)(2,1)S(1)}, s32[8,126]{1,0:T(8,128)S(1)}) custom-call(bf16[2,4,64,64,126]{4,3,2,1,0:T(8,128)(2,1)} %bitcast.6, s32[8,126]{1,0:T(8,128)} %bitcast.9, s32[1]{0:T(128)} %bitcast.4.device_ref), custom_call_target="tpu_custom_call" | custom-call | tf_op jit(solution)/shard_map/pallas_call | solution.py:181
  13.0 0.1 collective-permute-done.1.next_ref
  13.1 0.9 %collective-permute-done.near_ref = bf16[32,32,128]{2,1,0:T(8,128)(2,1)S(1)} collective-permute-done((bf16[32,32,128]{2,1,0:T(8,128)(2,1)S(1)}, bf16[32,32,128]{2,1,0:T(8,128)(2,1)S(1)}, u32[]{:S(2)}, u32[]{:S(2)}) %collective-permute-start) | collective-permute-done | bytes 262176 | tf_op jit(solution)/shard_map/ppermute | solution.py:389
  14.0 3.5 %shard_map.49 = (bf16[126,128,128]{2,1,0:T(8,128)(2,1)S(1)}, bf16[2,225,32,128]{3,2,1,0:T(8,128)(2,1)S(1)}, bf16[96,32,128]{2,1,0:T(8,128)(2,1)S(1)}) custom-call(bf16[2,4,64,64,126]{4,3,2,1,0:T(8,128)(2,1)} %bitcast.7, bf16[32,32,128]{2,1,0:T(8,128)(2,1)S(1)} %get-tuple-element.25.leaf_ref.own_ref, bf16[32,32,128]{2,1,0:T(8,128)(2,1)S(1)} %collective-permute-done.near_ref, ...), custom_call_target="tpu_custom_call" | custom-call | tf_op jit(solution)/shard_map/pallas_call | solution.py:242
  17.5 0.2 collective-permute-start.5
  17.7 2.1 %collective-permute-done.6.next_ref = bf16[31,32,128]{2,1,0:T(8,128)(2,1)S(1)} collective-permute-done((bf16[31,32,128]{2,1,0:T(8,128)(2,1)S(1)}, bf16[31,32,128]{2,1,0:T(8,128)(2,1)S(1)}, u32[]{:S(2)}, u32[]{:S(2)}) %collective-permute-start.6) | collective-permute-done | bytes 253984 | tf_op jit(solution)/shard_map/ppermute | solution.py:389
  19.8 0.7 %collective-permute-done.2.near_ref = bf16[31,32,128]{2,1,0:T(8,128)(2,1)S(1)} collective-permute-done((bf16[31,32,128]{2,1,0:T(8,128)(2,1)S(1)}, bf16[31,32,128]{2,1,0:T(8,128)(2,1)S(1)}, u32[]{:S(2)}, u32[]{:S(2)}) %collective-permute-start.2) | collective-permute-done | bytes 253984 | tf_op jit(solution)/shard_map/ppermute | solution.py:389
  20.5 0.3 shard_map.50
  20.8 0.1 collective-permute-start.7
  20.9 0.1 collective-permute-start.4
  21.0 0.3 collective-permute-start.3
  21.3 1.9 %collective-permute-done.7.upper_ref = bf16[93,32,128]{2,1,0:T(8,128)(2,1)S(1)} collective-permute-done((bf16[93,32,128]{2,1,0:T(8,128)(2,1)S(1)}, bf16[93,32,128]{2,1,0:T(8,128)(2,1)S(1)}, u32[]{:S(2)}, u32[]{:S(2)}) %collective-permute-start.7) | collective-permute-done | bytes 761888 | tf_op jit(solution)/shard_map/ppermute | solution.py:389
  23.1 0.0 collective-permute-done.5.leaf_ref
  23.1 0.6 %shard_map.51 = (bf16[2,225,32,128]{3,2,1,0:T(8,128)(2,1)S(1)}, bf16[2,218,32,128]{3,2,1,0:T(8,128)(2,1)S(1)}) custom-call(bf16[96,32,128]{2,1,0:T(8,128)(2,1)S(1)} %collective-permute-done.5.leaf_ref, bf16[93,32,128]{2,1,0:T(8,128)(2,1)S(1)} %collective-permute-done.7.upper_ref, ...), custom_call_target="tpu_custom_call", output_to_operand_aliasing={{0}: (2, {}), {1}: (3, {})} | custom-call | tf_op jit(solution)/shard_map/pallas_call | solution.py:273
  23.7 6.9 %collective-permute-done.4.far_ref = bf16[32,32,128]{2,1,0:T(8,128)(2,1)S(1)} collective-permute-done((bf16[32,32,128]{2,1,0:T(8,128)(2,1)S(1)}, bf16[32,32,128]{2,1,0:T(8,128)(2,1)S(1)}, u32[]{:S(2)}, u32[]{:S(2)}) %collective-permute-start.4) | collective-permute-done | bytes 262176 | tf_op jit(solution)/shard_map/ppermute | solution.py:389
  30.7 2.2 %shard_map.52 = (f32[32,32,128]{2,1,0:T(8,128)S(1)}, bf16[2,225,32,128]{3,2,1,0:T(8,128)(2,1)S(1)}) custom-call(s32[8,126]{1,0:T(8,128)S(1)} %get-tuple-element.30.place_ref, bf16[32,32,128]{2,1,0:T(8,128)(2,1)S(1)} %collective-permute-done.4.far_ref, bf16[126,128,128]{2,1,0:T(8,128)(2,1)S(1)} %get-tuple-element.31.first_ref, ...), custom_call_target="tpu_custom_call", output_to_operand_aliasing={{1}: (4, {})} | custom-call | tf_op jit(solution)/shard_map/pallas_call | solution.py:319
  32.8 0.6 %collective-permute-done.3.far_ref = bf16[31,32,128]{2,1,0:T(8,128)(2,1)S(1)} collective-permute-done((bf16[31,32,128]{2,1,0:T(8,128)(2,1)S(1)}, bf16[31,32,128]{2,1,0:T(8,128)(2,1)S(1)}, u32[]{:S(2)}, u32[]{:S(2)}) %collective-permute-start.3) | collective-permute-done | bytes 253984 | tf_op jit(solution)/shard_map/ppermute | solution.py:389
  33.4 3.8 %shard_map.53 = (f32[64,32,64]{2,1,0:T(8,128)}, bf16[2,218,32,128]{3,2,1,0:T(8,128)(2,1)S(1)}) custom-call(s32[8,126]{1,0:T(8,128)S(1)} %get-tuple-element.30.place_ref, bf16[31,32,128]{2,1,0:T(8,128)(2,1)S(1)} %collective-permute-done.3.far_ref, bf16[126,128,128]{2,1,0:T(8,128)(2,1)S(1)} %get-tuple-element.31.first_ref, ...), custom_call_target="tpu_custom_call", output_to_operand_aliasing={{1}: (6, {})} | custom-call | tf_op jit(solution)/shard_map/pallas_call | solution.py:366
Async XLA Ops:
  1.4 11.7 %collective-permute-start.1 = (bf16[32,32,128]{2,1,0:T(8,128)(2,1)S(1)}, bf16[32,32,128]{2,1,0:T(8,128)(2,1)}, u32[]{:S(2)}, u32[]{:S(2)}) collective-permute-start(bf16[32,32,128]{2,1,0:T(8,128)(2,1)S(1)} %get-tuple-element.25.leaf_ref.own_ref), channel_id=1, source_target_pairs={{0,16},{8,248},{16,32},{24,8},{32,48},{40,24},{48,64},{56,40},{64,... | collective-permute-start | bytes 786440 | tf_op jit(solution)/shard_map/ppermute | solution.py:389
  3.1 10.9 %collective-permute-start = (bf16[32,32,128]{2,1,0:T(8,128)(2,1)S(1)}, bf16[32,32,128]{2,1,0:T(8,128)(2,1)S(1)}, u32[]{:S(2)}, u32[]{:S(2)}) collective-permute-start(bf16[32,32,128]{2,1,0:T(8,128)(2,1)S(1)} %get-tuple-element.25.leaf_ref.own_ref), channel_id=1, source_target_pairs={{0,248},{8,16},{16,8},{24,32},{32,24},{40,48},{48,40},{56,64},{64,... | collective-permute-start | bytes 786440 | tf_op jit(solution)/shard_map/ppermute | solution.py:389
  8.1 11.7 %collective-permute-start.6 = (bf16[31,32,128]{2,1,0:T(8,128)(2,1)S(1)}, bf16[31,32,128]{2,1,0:T(8,128)(2,1)S(1)}, u32[]{:S(2)}, u32[]{:S(2)}) collective-permute-start(bf16[31,32,128]{2,1,0:T(8,128)(2,1)S(1)} %get-tuple-element.37.own_ref), channel_id=1, source_target_pairs={{0,16},{8,248},{16,32},{24,8},{32,48},{40,24},{48,64},{56,40},{64,... | collective-permute-start | bytes 761864 | tf_op jit(solution)/shard_map/ppermute | solution.py:389
  9.4 11.0 %collective-permute-start.2 = (bf16[31,32,128]{2,1,0:T(8,128)(2,1)S(1)}, bf16[31,32,128]{2,1,0:T(8,128)(2,1)S(1)}, u32[]{:S(2)}, u32[]{:S(2)}) collective-permute-start(bf16[31,32,128]{2,1,0:T(8,128)(2,1)S(1)} %get-tuple-element.37.own_ref), channel_id=1, source_target_pairs={{0,248},{8,16},{16,8},{24,32},{32,24},{40,48},{48,40},{56,64},{64,... | collective-permute-start | bytes 761864 | tf_op jit(solution)/shard_map/ppermute | solution.py:389
  17.5 5.7 %collective-permute-start.5 = (bf16[96,32,128]{2,1,0:T(8,128)(2,1)S(1)}, bf16[96,32,128]{2,1,0:T(8,128)(2,1)S(1)}, u32[]{:S(2)}, u32[]{:S(2)}) collective-permute-start(bf16[96,32,128]{2,1,0:T(8,128)(2,1)S(1)} %get-tuple-element.36), channel_id=1, source_target_pairs={{0,8},{8,0},{16,24},{24,16},{32,40},{40,32},{48,56},{56,48},{64,72... | collective-permute-start | bytes 2359304 | tf_op jit(solution)/shard_map/ppermute | solution.py:389
  20.8 2.3 %collective-permute-start.7 = (bf16[93,32,128]{2,1,0:T(8,128)(2,1)S(1)}, bf16[93,32,128]{2,1,0:T(8,128)(2,1)S(1)}, u32[]{:S(2)}, u32[]{:S(2)}) collective-permute-start(bf16[93,32,128]{2,1,0:T(8,128)(2,1)S(1)} %get-tuple-element.38), channel_id=1, source_target_pairs={{0,8},{8,0},{16,24},{24,16},{32,40},{40,32},{48,56},{56,48},{64,72... | collective-permute-start | bytes 2285576 | tf_op jit(solution)/shard_map/ppermute | solution.py:389
  20.9 9.8 %collective-permute-start.4 = (bf16[32,32,128]{2,1,0:T(8,128)(2,1)S(1)}, bf16[32,32,128]{2,1,0:T(8,128)(2,1)S(1)}, u32[]{:S(2)}, u32[]{:S(2)}) collective-permute-start(bf16[32,32,128]{2,1,0:T(8,128)(2,1)S(1)} %collective-permute-done.near_ref), channel_id=1, source_target_pairs={{0,16},{8,248},{16,32},{24,8},{32,48},{40,24},{48,64},{56,40},{64,... | collective-permute-start | bytes 786440 | tf_op jit(solution)/shard_map/ppermute | solution.py:389
  21.0 12.4 %collective-permute-start.3 = (bf16[31,32,128]{2,1,0:T(8,128)(2,1)S(1)}, bf16[31,32,128]{2,1,0:T(8,128)(2,1)S(1)}, u32[]{:S(2)}, u32[]{:S(2)}) collective-permute-start(bf16[31,32,128]{2,1,0:T(8,128)(2,1)S(1)} %collective-permute-done.2.near_ref), channel_id=1, source_target_pairs={{0,16},{8,248},{16,32},{24,8},{32,48},{40,24},{48,64},{56,40},{64,... | collective-permute-start | bytes 761864 | tf_op jit(solution)/shard_map/ppermute | solution.py:389
